TPU v7x, 32 devices: a whole 2x2x4 slice. The times are simulated.
32 devices in a mesh: gx: 2 (over x), gy: 4 (over z), gz: 4 (over y, core).
Axes of the slice: x: 2, y: 2, z: 4, core: 2. Of those that a mesh axis runs over, the one named last changes fastest.
Arguments:
- fluid_temp: float32 [32, 256, 512], P('gx', 'gy', 'gz'), may hold values from -6 to 6
- liquid: int32 [32, 256, 512], P('gx', 'gy', 'gz'), may hold values 0 or 1
- face_src: int32 [4, 4, 4, 128], P('gx', 'gy', 'gz'), may hold values from -1 to 131071, as said below
- face_dst: int32 [4, 4, 4, 128], P('gx', 'gy', 'gz'), may hold values from -1 to 1023, as said below
- solid_old: float32 [16, 16, 128], P(('gy', 'gz'), 'gx'), may hold values from -6 to 6
- solid_diag: float32 [16, 16, 128], P(('gy', 'gz'), 'gx'), may hold values from 4 to 16
- blocks: float32 [16, 16, 5, 128, 128], P(('gy', 'gz'), 'gx'), may hold values from -0.25 to 0.25
- pattern: int32 [16, 16, 5], P(('gy', 'gz'), 'gx'), may hold values 0 or 1
Outputs:
- fluid_new: float32 [32, 256, 512], P('gx', 'gy', 'gz')
- solid_temp: float32 [16, 16, 128], P(('gy', 'gz'), 'gx')
Inputs may be any that keep to these rules, and one draw needn't show every extreme that they name: `face_src`: entry q * 2 + r of slab (a, b) lists in its first c slots local cells of brick (q, a, b) whose temperatures go to run r, c from 1 to 128 and 128 in some blocks of every draw; the other slots hold -1; cells may repeat. `face_dst`: entry r * 2 + q of slab (a, b) names, slot by slot, the local solid cell of run r that receives the matching slot of face_src entry q * 2 + r, and -1 exactly where that slot of face_src is -1; cells may repeat.
All inputs are finite; a program needn't handle non-finite values. No bound on the sum of `liquid` or of `pattern` on one device may be relied on, other than what follows from the above.
Results may differ from a plain program's by a relative error of at most 0.00014.
Values sent between devices are 32-bit elements; how exact they have to be, the bound alone decides.
A program may use at most 64 MiB of HBM per device.

v0:
```python
import math

import jax
import jax.numpy as jnp
from jax import lax
from jax.sharding import PartitionSpec as P

REACH = 2
SWEEPS = 4
NB = 5


DIFFUSION = 0.12
EVAPORATION = 0.5
SATURATION = 0.25
WALL_COUPLING = 0.2


def padded_2(shard, sides, width, wrap):
    for axis, dim in sides:
        peers, length = (lax.axis_size(axis), shard.shape[dim])
        up = [(i, (i + 1) % peers) for i in range(peers if wrap else peers - 1)]
        down = [(j, i) for i, j in up]
        last = lax.slice_in_dim(shard, length - width, length, axis=dim)
        leading = lax.slice_in_dim(shard, 0, width, axis=dim)
        before = lax.ppermute(last, axis, up)
        after = lax.ppermute(leading, axis, down)
        shard = jnp.concatenate([before, shard, after], axis=dim)
    return shard


def apply_tiles(values, blocks_run, pattern_run, diagonal):
    tile_count = values.shape[0]
    padded = padded_2(values, (("gx", 0),), REACH, False)
    neighbours = jnp.stack([padded[offset : offset + tile_count] for offset in range(NB)], axis=1)
    neighbours = neighbours * pattern_run[:, :, None]
    coupled = jnp.einsum("tjab,tjb->ta", blocks_run, neighbours, precision=lax.Precision.HIGHEST)
    return diagonal * values + coupled


def chebyshev(right_side, blocks_run, pattern_run, diagonal):
    inverse = 1.0 / diagonal
    iterate = inverse * right_side
    residual = right_side - apply_tiles(iterate, blocks_run, pattern_run, diagonal)
    update = inverse * residual
    iterate = iterate + update
    rho_old = 0.5
    for sweep in range(1, SWEEPS):
        rho_next = 1.0 / (4.0 - rho_old)
        residual = right_side - apply_tiles(iterate, blocks_run, pattern_run, diagonal)
        update = rho_next * rho_old * update + 4.0 * rho_next * inverse * residual
        iterate = iterate + update
        rho_old = rho_next
    return iterate


def slot_hots(block_ids, row_count, width):
    valid = block_ids >= 0
    row_id = jnp.where(valid, block_ids // width, -1)
    depth = jnp.where(valid, block_ids % width, -1)
    row_hot = (row_id[:, None] == jnp.arange(row_count, dtype=jnp.int32)[None, :]).astype(
        jnp.float32
    )
    depth_hot = depth[:, None] == jnp.arange(width, dtype=jnp.int32)[None, :]
    return (row_hot, depth_hot)


def block_size(total):
    return math.gcd(total, 512)


def pick_cells(table, slot_ids):
    row_count, width = table.shape
    size = block_size(slot_ids.shape[0])

    def pick_one_block(block_ids):
        row_hot, depth_hot = slot_hots(block_ids, row_count, width)
        picked = jnp.dot(
            row_hot, table, precision=lax.Precision.HIGHEST, preferred_element_type=jnp.float32
        )
        return jnp.sum(jnp.where(depth_hot, picked, 0.0), axis=1)

    return lax.map(pick_one_block, slot_ids.reshape(-1, size)).reshape(-1)


def spread_cells(values, slot_ids, row_count, width):
    size = block_size(slot_ids.shape[0])

    def spread_one_block(total, operands):
        block_ids, block_values = operands
        row_hot, depth_hot = slot_hots(block_ids, row_count, width)
        placed = jnp.where(depth_hot, block_values[:, None], 0.0)
        added = jnp.dot(
            row_hot.T, placed, precision=lax.Precision.HIGHEST, preferred_element_type=jnp.float32
        )
        return (total + added, None)

    start = jnp.zeros((row_count, width), jnp.float32)
    total, unused = lax.scan(
        spread_one_block, start, (slot_ids.reshape(-1, size), values.reshape(-1, size))
    )
    return total


def per_device(fluid_temp, liquid, face_src, face_dst, solid_old, solid_diag, blocks, pattern):
    senders = lax.axis_size("gx")
    depth_count = fluid_temp.shape[2]
    row_count = fluid_temp.shape[0] * fluid_temp.shape[1]
    padded = padded_2(fluid_temp, (("gx", 0), ("gy", 1), ("gz", 2)), 1, True)
    source_ids = face_src.reshape(-1)
    fluid_table = fluid_temp.reshape(row_count, depth_count)
    outgoing = pick_cells(fluid_table, source_ids).reshape(senders, -1)
    arriving = lax.all_to_all(outgoing, "gx", split_axis=0, concat_axis=0, tiled=True)
    target_ids = face_dst.reshape(-1)
    tile_count = solid_old.shape[1]
    tile_width = solid_old.shape[2]
    gathered = spread_cells(arriving.reshape(-1), target_ids, tile_count, tile_width)
    diagonal = solid_diag[0]
    right_side = diagonal * solid_old[0] + gathered
    iterate = chebyshev(right_side, blocks[0], pattern[0].astype(jnp.float32), diagonal)
    sent_back = pick_cells(iterate, target_ids).reshape(senders, -1)
    returned = lax.all_to_all(sent_back, "gx", split_axis=0, concat_axis=0, tiled=True)
    centre = padded[1:-1, 1:-1, 1:-1]
    laplacian = padded[2:, 1:-1, 1:-1] + padded[:-2, 1:-1, 1:-1]
    laplacian = laplacian + padded[1:-1, 2:, 1:-1] + padded[1:-1, :-2, 1:-1]
    laplacian = laplacian + padded[1:-1, 1:-1, 2:] + padded[1:-1, 1:-1, :-2] - 6.0 * centre
    wall_sum = spread_cells((returned - outgoing).reshape(-1), source_ids, row_count, depth_count)
    wall_sum = wall_sum.reshape(fluid_temp.shape)
    liquid_share = liquid.astype(jnp.float32)
    fluid_new = (
        fluid_temp
        + DIFFUSION * laplacian
        - EVAPORATION * liquid_share * jnp.maximum(fluid_temp - SATURATION, 0.0)
        + WALL_COUPLING * wall_sum
    )
    return (fluid_new, iterate[None])


def solution(mesh):
    return jax.shard_map(
        per_device,
        mesh=mesh,
        in_specs=(
            P("gx", "gy", "gz"),
            P("gx", "gy", "gz"),
            P("gx", "gy", "gz", None),
            P("gx", "gy", "gz", None),
            P(("gy", "gz"), "gx", None),
            P(("gy", "gz"), "gx", None),
            P(("gy", "gz"), "gx", None, None, None),
            P(("gy", "gz"), "gx", None),
        ),
        out_specs=(P("gx", "gy", "gz"), P(("gy", "gz"), "gx", None)),
        check_vma=False,
    )
```

profile of v0, /device:TPU:0, one launch (start us, length us, event | category | flops | bytes accessed | tf_op | source)
XLA Modules:
  0.0 98.4 jit_solution(5652722390254571768)
XLA Ops:
  0.6 0.0 copy-start
  0.6 0.0 copy-start.4
  0.7 0.8 fusion.80
  1.5 2.3 %fusion.8 = f32[256]{0:T(256)} fusion(f32[1024,128]{1,0:T(8,128)} %bitcast.182, s32[256]{0:T(256)S(1)} %get-tuple-element.78, s32[256]{0:T(256)S(1)} %get-tuple-element.77), kind=kOutput, calls=%fused_computation.11 | convolution fusion | flops 403013376 | bytes 527360 | tf_op jit(solution)/shard_map/while/body/eval_jaxpr/dot_general | solution.py:78
  3.8 4.2 %all-to-all-start = ((f32[2,1,128]{2,1,0:T(1,128)}), f32[2,1,128]{2,1,0:T(1,128)S(1)}, u32[]{:S(2)}, u32[]{:S(2)}) async-start(f32[2,1,128]{2,1,0:T(1,128)} %bitcast.5), calls=%async_computation | async-start | bytes 2048 | tf_op jit(solution)/shard_map/all_to_all | solution.py:113
  8.0 0.7 fusion.81
  8.7 0.8 copy.71
  9.5 2.2 %all-to-all-done = f32[2,1,128]{2,1,0:T(1,128)S(1)} async-done(((f32[2,1,128]{2,1,0:T(1,128)}), f32[2,1,128]{2,1,0:T(1,128)S(1)}, u32[]{:S(2)}, u32[]{:S(2)}) %all-to-all-start) | async-done | bytes 1056 | tf_op jit(solution)/shard_map/all_to_all | solution.py:113
  11.7 1.0 fusion.79
  12.7 1.9 %collective-permute-start.6 = (f32[2,128]{1,0:T(2,128)S(1)}, f32[2,128]{1,0:T(2,128)S(1)}, u32[]{:S(2)}, u32[]{:S(2)}) collective-permute-start(f32[2,128]{1,0:T(2,128)S(1)} %get-tuple-element.74), channel_id=1, source_target_pairs={{0,16},{1,17},{2,18},{3,19},{4,20},{5,21},{6,22},{7,23},{8,24},{9,... | collective-permute-start | bytes 3080 | tf_op jit(solution)/shard_map/ppermute | solution.py:26
  14.6 0.1 copy.72
  14.7 1.3 %collective-permute-start.7 = (f32[2,128]{1,0:T(2,128)S(1)}, f32[2,128]{1,0:T(2,128)S(1)}, u32[]{:S(2)}, u32[]{:S(2)}) collective-permute-start(f32[2,128]{1,0:T(2,128)S(1)} %get-tuple-element.73), channel_id=1, source_target_pairs={{16,0},{17,1},{18,2},{19,3},{20,4},{21,5},{22,6},{23,7},{24,8},{25... | collective-permute-start | bytes 3080 | tf_op jit(solution)/shard_map/ppermute | solution.py:27
  16.0 0.0 collective-permute-done.6
  16.0 0.7 constant_dynamic-update-slice_fusion.5
  16.7 3.4 %collective-permute-done.7 = f32[2,128]{1,0:T(2,128)S(1)} collective-permute-done((f32[2,128]{1,0:T(2,128)S(1)}, f32[2,128]{1,0:T(2,128)S(1)}, u32[]{:S(2)}, u32[]{:S(2)}) %collective-permute-start.7) | collective-permute-done | bytes 1056 | tf_op jit(solution)/shard_map/ppermute | solution.py:27
  20.2 0.1 multiply_bitcast_fusion.3
  20.3 2.6 %fusion.6 = f32[8,1,128,1]{2,1,3,0:T(1,128)S(1)} fusion(f32[1,8,5,128,128]{4,3,2,1,0:T(8,128)S(1)} %copy-done, f32[8,5,128,1]{2,0,1,3:T(8,128)S(1)} %multiply_bitcast_fusion.3), kind=kOutput, calls=%fused_computation.6 | convolution fusion | flops 7864320 | bytes 2646016 | tf_op jit(solution)/shard_map/tjab,tjb->ta/dot_general | solution.py:37
  22.9 1.7 %collective-permute-start.8 = (f32[2,128]{1,0:T(2,128)S(1)}, f32[2,128]{1,0:T(2,128)S(1)}, u32[]{:S(2)}, u32[]{:S(2)}) collective-permute-start(f32[2,128]{1,0:T(2,128)S(1)} %get-tuple-element.72), channel_id=1, source_target_pairs={{0,16},{1,17},{2,18},{3,19},{4,20},{5,21},{6,22},{7,23},{8,24},{9,... | collective-permute-start | bytes 3080 | tf_op jit(solution)/shard_map/ppermute | solution.py:26
  24.6 1.3 %collective-permute-start.9 = (f32[2,128]{1,0:T(2,128)S(1)}, f32[2,128]{1,0:T(2,128)S(1)}, u32[]{:S(2)}, u32[]{:S(2)}) collective-permute-start(f32[2,128]{1,0:T(2,128)S(1)} %get-tuple-element.71), channel_id=1, source_target_pairs={{16,0},{17,1},{18,2},{19,3},{20,4},{21,5},{22,6},{23,7},{24,8},{25... | collective-permute-start | bytes 3080 | tf_op jit(solution)/shard_map/ppermute | solution.py:27
  25.9 0.0 collective-permute-done.8
  25.9 4.1 %collective-permute-done.9 = f32[2,128]{1,0:T(2,128)S(1)} collective-permute-done((f32[2,128]{1,0:T(2,128)S(1)}, f32[2,128]{1,0:T(2,128)S(1)}, u32[]{:S(2)}, u32[]{:S(2)}) %collective-permute-start.9) | collective-permute-done | bytes 1056 | tf_op jit(solution)/shard_map/ppermute | solution.py:27
  30.1 0.1 multiply_bitcast_fusion.2
  30.1 2.6 %fusion.4 = f32[8,1,128,1]{2,1,3,0:T(1,128)S(1)} fusion(f32[1,8,5,128,128]{4,3,2,1,0:T(8,128)S(1)} %copy-done, f32[8,5,128,1]{2,0,1,3:T(8,128)S(1)} %multiply_bitcast_fusion.2), kind=kOutput, calls=%fused_computation.4 | convolution fusion | flops 7864320 | bytes 2646016 | tf_op jit(solution)/shard_map/tjab,tjb->ta/dot_general | solution.py:37
  32.8 1.7 %collective-permute-start.10 = (f32[2,128]{1,0:T(2,128)S(1)}, f32[2,128]{1,0:T(2,128)S(1)}, u32[]{:S(2)}, u32[]{:S(2)}) collective-permute-start(f32[2,128]{1,0:T(2,128)S(1)} %get-tuple-element.70), channel_id=1, source_target_pairs={{0,16},{1,17},{2,18},{3,19},{4,20},{5,21},{6,22},{7,23},{8,24},{9,... | collective-permute-start | bytes 3080 | tf_op jit(solution)/shard_map/ppermute | solution.py:26
  34.5 1.3 %collective-permute-start.11 = (f32[2,128]{1,0:T(2,128)S(1)}, f32[2,128]{1,0:T(2,128)S(1)}, u32[]{:S(2)}, u32[]{:S(2)}) collective-permute-start(f32[2,128]{1,0:T(2,128)S(1)} %get-tuple-element.69), channel_id=1, source_target_pairs={{16,0},{17,1},{18,2},{19,3},{20,4},{21,5},{22,6},{23,7},{24,8},{25... | collective-permute-start | bytes 3080 | tf_op jit(solution)/shard_map/ppermute | solution.py:27
  35.8 0.0 collective-permute-done.10
  35.8 4.1 %collective-permute-done.11 = f32[2,128]{1,0:T(2,128)S(1)} collective-permute-done((f32[2,128]{1,0:T(2,128)S(1)}, f32[2,128]{1,0:T(2,128)S(1)}, u32[]{:S(2)}, u32[]{:S(2)}) %collective-permute-start.11) | collective-permute-done | bytes 1056 | tf_op jit(solution)/shard_map/ppermute | solution.py:27
  39.9 0.1 multiply_bitcast_fusion.1
  40.0 2.6 %fusion.2 = f32[8,1,128,1]{2,1,3,0:T(1,128)S(1)} fusion(f32[1,8,5,128,128]{4,3,2,1,0:T(8,128)S(1)} %copy-done, f32[8,5,128,1]{2,0,1,3:T(8,128)S(1)} %multiply_bitcast_fusion.1), kind=kOutput, calls=%fused_computation.2 | convolution fusion | flops 7864320 | bytes 2646016 | tf_op jit(solution)/shard_map/tjab,tjb->ta/dot_general | solution.py:37
  42.7 1.7 %collective-permute-start.12 = (f32[2,128]{1,0:T(2,128)S(1)}, f32[2,128]{1,0:T(2,128)S(1)}, u32[]{:S(2)}, u32[]{:S(2)}) collective-permute-start(f32[2,128]{1,0:T(2,128)S(1)} %get-tuple-element.68), channel_id=1, source_target_pairs={{0,16},{1,17},{2,18},{3,19},{4,20},{5,21},{6,22},{7,23},{8,24},{9,... | collective-permute-start | bytes 3080 | tf_op jit(solution)/shard_map/ppermute | solution.py:26
  44.4 0.1 collective-permute-start.1
  44.4 2.0 %collective-permute-start = (f32[1,64,128]{2,1,0:T(8,128)S(1)}, f32[1,64,128]{2,1,0:T(8,128)S(1)}, u32[]{:S(2)}, u32[]{:S(2)}) collective-permute-start(f32[1,64,128]{2,1,0:T(8,128)S(1)} %get-tuple-element.65), channel_id=1, source_target_pairs={{16,0},{0,16},{17,1},{1,17},{18,2},{2,18},{19,3},{3,19},{20,4},{4,... | collective-permute-start | bytes 98312 | tf_op jit(solution)/shard_map/ppermute | solution.py:27
  46.4 1.3 %collective-permute-start.13 = (f32[2,128]{1,0:T(2,128)S(1)}, f32[2,128]{1,0:T(2,128)S(1)}, u32[]{:S(2)}, u32[]{:S(2)}) collective-permute-start(f32[2,128]{1,0:T(2,128)S(1)} %get-tuple-element.67), channel_id=1, source_target_pairs={{16,0},{17,1},{18,2},{19,3},{20,4},{21,5},{22,6},{23,7},{24,8},{25... | collective-permute-start | bytes 3080 | tf_op jit(solution)/shard_map/ppermute | solution.py:27
  47.7 0.0 collective-permute-done.12
  47.8 4.1 %collective-permute-done.13 = f32[2,128]{1,0:T(2,128)S(1)} collective-permute-done((f32[2,128]{1,0:T(2,128)S(1)}, f32[2,128]{1,0:T(2,128)S(1)}, u32[]{:S(2)}, u32[]{:S(2)}) %collective-permute-start.13) | collective-permute-done | bytes 1056 | tf_op jit(solution)/shard_map/ppermute | solution.py:27
  51.9 0.1 multiply_bitcast_fusion
  52.0 2.6 %fusion = f32[8,1,128,1]{2,1,3,0:T(1,128)S(1)} fusion(f32[1,8,5,128,128]{4,3,2,1,0:T(8,128)S(1)} %copy-done, f32[8,5,128,1]{2,0,1,3:T(8,128)S(1)} %multiply_bitcast_fusion), kind=kOutput, calls=%fused_computation | convolution fusion | flops 7864320 | bytes 2646016 | tf_op jit(solution)/shard_map/tjab,tjb->ta/dot_general | solution.py:37
  54.6 0.0 copy-start.5
  54.6 0.0 collective-permute-done.1
  54.7 0.0 collective-permute-done
  54.7 1.2 %pad_maximum_fusion.8 = (f32[16,64,128]{2,1,0:T(8,128)}, f32[18,64,128]{2,1,0:T(8,128)S(1)}, f32[16,64,128]{2,1,0:T(8,128)}) fusion(f32[16,64,128]{2,1,0:T(8,128)S(1)} %copy-done.1, f32[1,64,128]{2,1,0:T(8,128)S(1)} %collective-permute-done.1, f32[18,64,128]{2,1,0:T(8,128)S(1)} %constant_dynamic-update-slice_fusion.2, f32[1,64,128]{2,1,0:T(8,128)S(1)} %collective-permute-done), kind=kLoop, calls=%fused_computation.33 | loop fusion | flops 262144 | bytes 2162688 | tf_op jit(solution)/shard_map/concatenate | solution.py:28
  55.9 0.8 copy-done.3
  56.7 4.1 %collective-permute-start.2 = (f32[18,1,128]{2,0,1:T(8,128)S(1)}, f32[18,1,128]{2,0,1:T(8,128)S(1)}, u32[]{:S(2)}, u32[]{:S(2)}) collective-permute-start(f32[18,1,128]{2,0,1:T(8,128)S(1)} %copy.85), channel_id=1, source_target_pairs={{4,0},{8,4},{12,8},{0,12},{5,1},{9,5},{13,9},{1,13},{6,2},{10,6},{... | collective-permute-start | bytes 27656 | tf_op jit(solution)/shard_map/ppermute | solution.py:27
  60.8 0.0 collective-permute-start.3
  60.8 0.8 fusion.9
  61.7 3.3 %all-to-all-start.1 = ((f32[2,1,128]{2,1,0:T(1,128)}), f32[2,1,128]{2,1,0:T(1,128)S(1)}, u32[]{:S(2)}, u32[]{:S(2)}) async-start(f32[2,1,128]{2,1,0:T(1,128)} %bitcast.41), calls=%async_computation.1 | async-start | bytes 2048 | tf_op jit(solution)/shard_map/all_to_all | solution.py:122
  65.0 1.4 %copy.68 = f32[16,64,128]{1,0,2:T(8,128)} copy(f32[16,64,128]{2,1,0:T(8,128)S(1)} %copy-done.1) | data formatting | bytes 1048576 | tf_op args[0]
  66.4 2.4 %copy.69 = s32[16,64,128]{1,0,2:T(8,128)} copy(s32[16,64,128]{2,1,0:T(8,128)} %param.9) | data formatting | bytes 1048576 | tf_op args[1]
  68.8 0.0 all-to-all-done.1
  68.8 0.7 sub.60
  69.5 2.7 %copy.59 = f32[18,64,128]{1,0,2:T(8,128)} copy(f32[18,64,128]{2,1,0:T(8,128)} %copy-done.3) | data formatting | bytes 1179648 | tf_op jit(solution)/shard_map/concatenate | solution.py:28
  72.3 0.0 collective-permute-done.2
  72.3 1.7 %copy.60 = f32[18,1,128]{1,0,2:T(8,128)} copy(f32[18,1,128]{2,0,1:T(8,128)S(1)} %collective-permute-done.2) | data formatting | bytes 18432 | tf_op jit(solution)/shard_map/ppermute | solution.py:27
  73.9 0.0 collective-permute-done.3
  73.9 1.7 %copy.62 = f32[18,1,128]{1,0,2:T(8,128)} copy(f32[18,1,128]{2,0,1:T(8,128)S(1)} %collective-permute-done.3) | data formatting | bytes 18432 | tf_op jit(solution)/shard_map/ppermute | solution.py:26
  75.6 0.9 pad_maximum_fusion.12
  76.5 0.1 collective-permute-start.4
  76.5 0.5 collective-permute-start.5
  77.0 1.6 %convolution_multiply_fusion = f32[1024,128]{1,0:T(8,128)} fusion(s32[256]{0:T(256)S(1)} %get-tuple-element.78, f32[256]{0:T(256)S(1)} %sub.60, s32[256]{0:T(256)S(1)} %get-tuple-element.77), kind=kOutput, calls=%fused_computation.8 | convolution fusion | flops 403374080 | bytes 527360 | tf_op jit(solution)/shard_map/while/body/eval_jaxpr/dot_general | solution.py:93
  78.6 2.4 %copy.73 = f32[16,64,128]{1,0,2:T(8,128)} copy(f32[16,64,128]{2,1,0:T(8,128)} %bitcast.183) | data formatting | bytes 1048576 | tf_op jit(solution)/shard_map/mul | solution.py:134
  81.0 2.4 %copy.83 = f32[16,64,128]{1,0,2:T(8,128)} copy(f32[16,64,128]{2,1,0:T(8,128)} %get-tuple-element.64) | data formatting | bytes 1048576
  83.5 1.5 %copy.84 = f32[16,64,128]{1,0,2:T(8,128)} copy(f32[16,64,128]{2,1,0:T(8,128)S(1)} %copy-done.2) | data formatting | bytes 1048576
  84.9 11.1 %fusion.15 = f32[16,64,128]{1,0,2:T(8,128)} fusion(f32[16,64,128]{1,0,2:T(8,128)} %copy.73, f32[16,64,128]{1,0,2:T(8,128)} %copy.68, f32[18,66,1]{1,0,2:T(8,128)S(1)} %collective-permute-done.5, f32[18,1,128]{1,0,2:T(8,128)} %copy.60, f32[18,64,128]{1,0,2:T(8,128)} %copy.59, f32[18,1,128]{1,0,2:T(8,128)} %copy.62, ...), kind=kLoop, calls=%fused_computation.20 | loop fusion | flops 3145728 | bytes 3763488 | tf_op jit(solution)/shard_map/add | solution.py:131
  96.0 2.4 %copy.74 = f32[16,64,128]{2,1,0:T(8,128)} copy(f32[16,64,128]{1,0,2:T(8,128)} %fusion.15) | data formatting | bytes 1048576
  (44 shorter events, 0.3 us)
Async XLA Ops:
  0.6 19.6 %copy-start = (f32[1,8,5,128,128]{4,3,2,1,0:T(8,128)S(1)}, f32[1,8,5,128,128]{4,3,2,1,0:T(8,128)}, u32[]{:S(2)}) copy-start(f32[1,8,5,128,128]{4,3,2,1,0:T(8,128)} %param.14) | copy-start | bytes 7864324
  0.6 22.2 %copy-start.4 = (f32[1,8,128]{2,1,0:T(8,128)S(1)}, f32[1,8,128]{2,1,0:T(8,128)}, u32[]{:S(2)}) copy-start(f32[1,8,128]{2,1,0:T(8,128)} %param.13) | copy-start | bytes 12292
  3.8 7.9 %all-to-all-start = ((f32[2,1,128]{2,1,0:T(1,128)}), f32[2,1,128]{2,1,0:T(1,128)S(1)}, u32[]{:S(2)}, u32[]{:S(2)}) async-start(f32[2,1,128]{2,1,0:T(1,128)} %bitcast.5), calls=%async_computation | async-start | bytes 2048 | tf_op jit(solution)/shard_map/all_to_all | solution.py:113
  12.7 3.3 %collective-permute-start.6 = (f32[2,128]{1,0:T(2,128)S(1)}, f32[2,128]{1,0:T(2,128)S(1)}, u32[]{:S(2)}, u32[]{:S(2)}) collective-permute-start(f32[2,128]{1,0:T(2,128)S(1)} %get-tuple-element.74), channel_id=1, source_target_pairs={{0,16},{1,17},{2,18},{3,19},{4,20},{5,21},{6,22},{7,23},{8,24},{9,... | collective-permute-start | bytes 3080 | tf_op jit(solution)/shard_map/ppermute | solution.py:26
  14.7 5.5 %collective-permute-start.7 = (f32[2,128]{1,0:T(2,128)S(1)}, f32[2,128]{1,0:T(2,128)S(1)}, u32[]{:S(2)}, u32[]{:S(2)}) collective-permute-start(f32[2,128]{1,0:T(2,128)S(1)} %get-tuple-element.73), channel_id=1, source_target_pairs={{16,0},{17,1},{18,2},{19,3},{20,4},{21,5},{22,6},{23,7},{24,8},{25... | collective-permute-start | bytes 3080 | tf_op jit(solution)/shard_map/ppermute | solution.py:27
  22.9 3.0 %collective-permute-start.8 = (f32[2,128]{1,0:T(2,128)S(1)}, f32[2,128]{1,0:T(2,128)S(1)}, u32[]{:S(2)}, u32[]{:S(2)}) collective-permute-start(f32[2,128]{1,0:T(2,128)S(1)} %get-tuple-element.72), channel_id=1, source_target_pairs={{0,16},{1,17},{2,18},{3,19},{4,20},{5,21},{6,22},{7,23},{8,24},{9,... | collective-permute-start | bytes 3080 | tf_op jit(solution)/shard_map/ppermute | solution.py:26
  24.6 5.5 %collective-permute-start.9 = (f32[2,128]{1,0:T(2,128)S(1)}, f32[2,128]{1,0:T(2,128)S(1)}, u32[]{:S(2)}, u32[]{:S(2)}) collective-permute-start(f32[2,128]{1,0:T(2,128)S(1)} %get-tuple-element.71), channel_id=1, source_target_pairs={{16,0},{17,1},{18,2},{19,3},{20,4},{21,5},{22,6},{23,7},{24,8},{25... | collective-permute-start | bytes 3080 | tf_op jit(solution)/shard_map/ppermute | solution.py:27
  30.1 14.2 %copy-start.1 = (f32[16,64,128]{2,1,0:T(8,128)S(1)}, f32[16,64,128]{2,1,0:T(8,128)}, u32[]{:S(2)}) copy-start(f32[16,64,128]{2,1,0:T(8,128)} %param.8) | copy-start | bytes 1572868
  32.8 3.0 %collective-permute-start.10 = (f32[2,128]{1,0:T(2,128)S(1)}, f32[2,128]{1,0:T(2,128)S(1)}, u32[]{:S(2)}, u32[]{:S(2)}) collective-permute-start(f32[2,128]{1,0:T(2,128)S(1)} %get-tuple-element.70), channel_id=1, source_target_pairs={{0,16},{1,17},{2,18},{3,19},{4,20},{5,21},{6,22},{7,23},{8,24},{9,... | collective-permute-start | bytes 3080 | tf_op jit(solution)/shard_map/ppermute | solution.py:26
  34.5 5.5 %collective-permute-start.11 = (f32[2,128]{1,0:T(2,128)S(1)}, f32[2,128]{1,0:T(2,128)S(1)}, u32[]{:S(2)}, u32[]{:S(2)}) collective-permute-start(f32[2,128]{1,0:T(2,128)S(1)} %get-tuple-element.69), channel_id=1, source_target_pairs={{16,0},{17,1},{18,2},{19,3},{20,4},{21,5},{22,6},{23,7},{24,8},{25... | collective-permute-start | bytes 3080 | tf_op jit(solution)/shard_map/ppermute | solution.py:27
  42.7 5.1 %collective-permute-start.12 = (f32[2,128]{1,0:T(2,128)S(1)}, f32[2,128]{1,0:T(2,128)S(1)}, u32[]{:S(2)}, u32[]{:S(2)}) collective-permute-start(f32[2,128]{1,0:T(2,128)S(1)} %get-tuple-element.68), channel_id=1, source_target_pairs={{0,16},{1,17},{2,18},{3,19},{4,20},{5,21},{6,22},{7,23},{8,24},{9,... | collective-permute-start | bytes 3080 | tf_op jit(solution)/shard_map/ppermute | solution.py:26
  44.4 10.3 %collective-permute-start.1 = (f32[1,64,128]{2,1,0:T(8,128)S(1)}, f32[1,64,128]{2,1,0:T(8,128)S(1)}, u32[]{:S(2)}, u32[]{:S(2)}) collective-permute-start(f32[1,64,128]{2,1,0:T(8,128)S(1)} %get-tuple-element.66), channel_id=1, source_target_pairs={{0,16},{16,0},{1,17},{17,1},{2,18},{18,2},{3,19},{19,3},{4,20},{20... | collective-permute-start | bytes 98312 | tf_op jit(solution)/shard_map/ppermute | solution.py:26
  44.4 10.2 %collective-permute-start = (f32[1,64,128]{2,1,0:T(8,128)S(1)}, f32[1,64,128]{2,1,0:T(8,128)S(1)}, u32[]{:S(2)}, u32[]{:S(2)}) collective-permute-start(f32[1,64,128]{2,1,0:T(8,128)S(1)} %get-tuple-element.65), channel_id=1, source_target_pairs={{16,0},{0,16},{17,1},{1,17},{18,2},{2,18},{19,3},{3,19},{20,4},{4,... | collective-permute-start | bytes 98312 | tf_op jit(solution)/shard_map/ppermute | solution.py:27
  46.4 5.5 %collective-permute-start.13 = (f32[2,128]{1,0:T(2,128)S(1)}, f32[2,128]{1,0:T(2,128)S(1)}, u32[]{:S(2)}, u32[]{:S(2)}) collective-permute-start(f32[2,128]{1,0:T(2,128)S(1)} %get-tuple-element.67), channel_id=1, source_target_pairs={{16,0},{17,1},{18,2},{19,3},{20,4},{21,5},{22,6},{23,7},{24,8},{25... | collective-permute-start | bytes 3080 | tf_op jit(solution)/shard_map/ppermute | solution.py:27
  54.6 14.2 %copy-start.5 = (f32[8,128]{1,0:T(8,128)}, f32[8,128]{1,0:T(8,128)S(1)}, u32[]{:S(2)}) copy-start(f32[8,128]{1,0:T(8,128)S(1)} %fusion.78) | copy-start | bytes 12292
  55.9 0.8 copy-start.3
  56.7 15.5 %collective-permute-start.2 = (f32[18,1,128]{2,0,1:T(8,128)S(1)}, f32[18,1,128]{2,0,1:T(8,128)S(1)}, u32[]{:S(2)}, u32[]{:S(2)}) collective-permute-start(f32[18,1,128]{2,0,1:T(8,128)S(1)} %copy.85), channel_id=1, source_target_pairs={{4,0},{8,4},{12,8},{0,12},{5,1},{9,5},{13,9},{1,13},{6,2},{10,6},{... | collective-permute-start | bytes 27656 | tf_op jit(solution)/shard_map/ppermute | solution.py:27
  60.8 13.1 %collective-permute-start.3 = (f32[18,1,128]{2,0,1:T(8,128)S(1)}, f32[18,1,128]{2,0,1:T(8,128)S(1)}, u32[]{:S(2)}, u32[]{:S(2)}) collective-permute-start(f32[18,1,128]{2,0,1:T(8,128)S(1)} %copy.86), channel_id=1, source_target_pairs={{0,4},{4,8},{8,12},{12,0},{1,5},{5,9},{9,13},{13,1},{2,6},{6,10},{... | collective-permute-start | bytes 27656 | tf_op jit(solution)/shard_map/ppermute | solution.py:26
  61.7 7.1 %all-to-all-start.1 = ((f32[2,1,128]{2,1,0:T(1,128)}), f32[2,1,128]{2,1,0:T(1,128)S(1)}, u32[]{:S(2)}, u32[]{:S(2)}) async-start(f32[2,1,128]{2,1,0:T(1,128)} %bitcast.41), calls=%async_computation.1 | async-start | bytes 2048 | tf_op jit(solution)/shard_map/all_to_all | solution.py:122
  76.5 7.0 %copy-start.2 = (f32[16,64,128]{2,1,0:T(8,128)S(1)}, f32[16,64,128]{2,1,0:T(8,128)}, u32[]{:S(2)}) copy-start(f32[16,64,128]{2,1,0:T(8,128)} %get-tuple-element.58) | copy-start | bytes 1572868
  76.5 8.4 %collective-permute-start.4 = (f32[18,66,1]{1,0,2:T(8,128)S(1)}, f32[18,66,1]{1,0,2:T(8,128)S(1)}, u32[]{:S(2)}, u32[]{:S(2)}) collective-permute-start(f32[18,66,1]{1,0,2:T(8,128)S(1)} %get-tuple-element.50), channel_id=1, source_target_pairs={{1,0},{2,1},{3,2},{0,3},{5,4},{6,5},{7,6},{4,7},{9,8},{10,9},{11,1... | collective-permute-start | bytes 14264 | tf_op jit(solution)/shard_map/ppermute | solution.py:27
  76.5 8.4 %collective-permute-start.5 = (f32[18,66,1]{1,0,2:T(8,128)S(1)}, f32[18,66,1]{1,0,2:T(8,128)S(1)}, u32[]{:S(2)}, u32[]{:S(2)}) collective-permute-start(f32[18,66,1]{1,0,2:T(8,128)S(1)} %get-tuple-element.51), channel_id=1, source_target_pairs={{0,1},{1,2},{2,3},{3,0},{4,5},{5,6},{6,7},{7,4},{8,9},{9,10},{10,1... | collective-permute-start | bytes 14264 | tf_op jit(solution)/shard_map/ppermute | solution.py:26
where the time goes:
time: 100 us; the launch traced here: 98.4 us
  starting transfers between devices  26.3 us (26%)
  local copies, waits for them, and re-layouts  20.4 us (20%)
  waiting for transfers between devices  18 us (18%)
  other arithmetic  16.6 us (17%)
  matrix products  16.2 us (16%)
  between operations  1.01 us (1%)
    ppermute x7, waiting for transfers between devices, padded_2(): after = lax.ppermute(leading, axis, down)  15.8 us
    unnamed x24, local copies, waits for them, and re-layouts  11.7 us
    ppermute x7, starting transfers between devices, padded_2(): after = lax.ppermute(leading, axis, down)  11.3 us
    add x1, other arithmetic, per_device(): fluid_temp + DIFFUSION * laplacian  11.1 us
    dot_general x4, matrix products, apply_tiles(): jnp.einsum('tjab,tjb->ta', blocks_run, neighbours, precision=lax.Precisio...  10.4 us
    ppermute x7, starting transfers between devices, padded_2(): before = lax.ppermute(last, axis, up)  7.47 us
    all_to_all x1, starting transfers between devices, per_device(): lax.all_to_all(outgoing, 'gx', split_axis=0, concat_axis=0, tiled=True)  4.21 us
    all_to_all x1, starting transfers between devices, per_device(): lax.all_to_all(sent_back, 'gx', split_axis=0, concat_axis=0, tiled=True)  3.29 us
  transfers between devices with their start and end apart: 16, of which 5 were waited for; matrix products, arithmetic and copies ran while one was open for 23% of the time, Pallas kernels for 0%

commit v1 on v0

v1 whole, which is shorter than its diff:
```python
import functools

import jax
import jax.numpy as jnp
from jax import lax
from jax.experimental import pallas as pl
from jax.experimental.pallas import tpu as pltpu
from jax.sharding import PartitionSpec as P

REACH = 2
SWEEPS = 4
NB = 5
DIFFUSION = 0.12
EVAPORATION = 0.5
SATURATION = 0.25
WALL_COUPLING = 0.2
MESH = pl.DeviceIdType.MESH
F32 = jnp.float32
BF16 = jnp.bfloat16


def split(values):
    high = values.astype(BF16)
    return high, (values - high.astype(F32)).astype(BF16)


def dot(a, b):
    return jnp.dot(a, b, preferred_element_type=F32)


def dot_nt(a, b):
    return lax.dot_general(a, b, (((1,), (1,)), ((), ())), preferred_element_type=F32)


def rows_of(shape):
    return lax.broadcasted_iota(jnp.int32, shape, 0)


def repeat(count, body):
    if count == 1:
        body(0)
    else:
        pl.loop(0, count)(body)


def kernel(
    senders, group,
    fluid_h, liquid_h, src_h, dst_h, old_h, diag_h, blocks_h, pat_h,
    new_ref, solid_ref,
    fluid, liquid, src, dst, old, diag, blocks, pat,
    hot, table, base, outp, arr, sent, ret, pre_out, pre_in, halo_out, halo,
    x_in, y_out, y_in, z_out, z_in, ext, gather, win, sums,
    load_sem, arr_send, arr_recv, ret_send, ret_recv, pre_send, pre_recv,
    halo_send, halo_recv, face_send, face_recv,
):
    cx, cy, cz = fluid.shape
    rows = cx * cy
    tiles, width = old.shape[1], old.shape[2]
    chunks = senders // group
    me = lax.axis_index("gx")
    gy, gz = lax.axis_index("gy"), lax.axis_index("gz")
    ny, nz = lax.axis_size("gy"), lax.axis_size("gz")
    left, right = lax.rem(me + senders - 1, senders), lax.rem(me + 1, senders)
    below, above = lax.rem(gy + ny - 1, ny), lax.rem(gy + 1, ny)
    before, after = lax.rem(gz + nz - 1, nz), lax.rem(gz + 1, nz)
    has_left, has_right = me > 0, me < senders - 1

    barrier = pltpu.get_barrier_semaphore()
    peers = [{"gx": lax.rem(me + d, senders)} for d in range(1, senders)]
    peers += [{"gy": below}, {"gy": above}, {"gz": before}, {"gz": after}]
    for peer in peers:
        pl.semaphore_signal(barrier, inc=1, device_id=peer, device_id_type=MESH)

    pairs = [(src_h, src), (fluid_h, fluid), (dst_h, dst), (old_h, old), (diag_h, diag),
             (pat_h, pat), (blocks_h, blocks), (liquid_h, liquid)]
    loads = [pltpu.make_async_copy(a, b, load_sem.at[i]) for i, (a, b) in enumerate(pairs)]
    for load in loads:
        load.start()

    def send(source, target, send_sem, recv_sem, device):
        return pltpu.make_async_remote_copy(
            src_ref=source, dst_ref=target, send_sem=send_sem, recv_sem=recv_sem,
            device_id=device, device_id_type=MESH)

    outp[...] = jnp.zeros_like(outp)
    ext[...] = jnp.zeros_like(ext)
    loads[0].wait()

    def make_hot(c):
        for j in range(group):
            ids = src[c * group + j, 0]
            row = ids >> 7
            for s in range(0, rows, 128):
                hit = rows_of((128, width)) + s == row
                hot[c, s:s + 128, j * width:(j + 1) * width] = jnp.where(hit, 1.0, 0.0).astype(BF16)

    repeat(chunks, make_hot)

    for load in loads[2:5]:
        load.wait()
    diagonal = diag[0]
    inverse = 1.0 / diagonal
    fixed = diagonal * old[0]
    for side, lo in ((0, 0), (1, tiles - REACH)):
        for q in range(senders):
            pre_out[side, q:q + 1, :] = dst[q, 0].astype(F32)
        pre_out[side, senders:senders + REACH, :] = fixed[lo:lo + REACH]
        pre_out[side, senders + REACH:senders + 2 * REACH, :] = inverse[lo:lo + REACH]
    pl.semaphore_wait(barrier, len(peers))

    pre_l = send(pre_out.at[0], pre_in.at[1], pre_send.at[0], pre_recv.at[1], {"gx": left})
    pre_r = send(pre_out.at[1], pre_in.at[0], pre_send.at[1], pre_recv.at[0], {"gx": right})
    halo_l = [send(halo_out.at[k, 0], halo.at[k, 1], halo_send.at[k, 0], halo_recv.at[k, 1],
                   {"gx": left}) for k in range(SWEEPS - 1)]
    halo_r = [send(halo_out.at[k, 1], halo.at[k, 0], halo_send.at[k, 1], halo_recv.at[k, 0],
                   {"gx": right}) for k in range(SWEEPS - 1)]

    @pl.when(has_left)
    def _():
        pre_l.start()

    @pl.when(has_right)
    def _():
        pre_r.start()

    @pl.when(jnp.logical_not(has_left))
    def _():
        pre_in[0] = jnp.zeros_like(pre_in[0])
        for k in range(SWEEPS - 1):
            halo[k, 0] = jnp.zeros_like(halo[k, 0])

    @pl.when(jnp.logical_not(has_right))
    def _():
        pre_in[1] = jnp.zeros_like(pre_in[1])
        for k in range(SWEEPS - 1):
            halo[k, 1] = jnp.zeros_like(halo[k, 1])

    loads[1].wait()
    per = 128 // cy
    for s in range(rows // 128):
        flipped = fluid[s * per:(s + 1) * per].reshape(128, cz).T
        high, low = split(flipped)
        table[0:cz, s * 128:(s + 1) * 128] = high
        table[cz:2 * cz, s * 128:(s + 1) * 128] = low
        z_out[0, :, s * 128:(s + 1) * 128] = flipped[0:1]
        z_out[1, :, s * 128:(s + 1) * 128] = flipped[cz - 1:cz]

    def pick(c):
        picked = dot(table[...], hot[c])
        picked = picked[0:cz] + picked[cz:2 * cz]
        for j in range(group):
            depth = src[c * group + j, 0] & (cz - 1)
            part = picked[:, j * width:(j + 1) * width]
            part = jnp.where(rows_of((cz, width)) == depth, part, 0.0)
            outp[c * group + j + 1] = jnp.sum(part, axis=0, keepdims=True)

    repeat(chunks, pick)
    arrivals = []
    for d in range(1, senders):
        peer = lax.rem(me + d, senders)
        arrivals.append(send(outp.at[pl.ds(peer, 3)], arr.at[me], arr_send.at[d], arr_recv.at[d],
                             {"gx": peer}))
        arrivals[-1].start()
    arr[pl.ds(me, 1)] = outp[pl.ds(me, 3)][None]

    y_out[0] = fluid[:, 0, :]
    y_out[1] = fluid[:, cy - 1, :]
    faces = [
        send(fluid.at[0], x_in.at[1], face_send.at[0], face_recv.at[0], {"gx": left}),
        send(fluid.at[cx - 1], x_in.at[0], face_send.at[1], face_recv.at[1], {"gx": right}),
        send(y_out.at[0], y_in.at[1], face_send.at[2], face_recv.at[2], {"gy": below}),
        send(y_out.at[1], y_in.at[0], face_send.at[3], face_recv.at[3], {"gy": above}),
        send(z_out.at[0], z_in.at[1], face_send.at[4], face_recv.at[4], {"gz": before}),
        send(z_out.at[1], z_in.at[0], face_send.at[5], face_recv.at[5], {"gz": after}),
    ]
    for face in faces:
        face.start()

    loads[7].wait()
    lane = lax.broadcasted_iota(jnp.int32, (cy, cz), 1)
    line = lax.broadcasted_iota(jnp.int32, (cy, cz), 0)
    for i in range(cx):
        here = fluid[i]
        near = jnp.where(line == 0, 0.0, pltpu.roll(here, 1, 0))
        near = near + jnp.where(line == cy - 1, 0.0, pltpu.roll(here, cy - 1, 0))
        near = near + jnp.where(lane == 0, 0.0, pltpu.roll(here, 1, 1))
        near = near + jnp.where(lane == cz - 1, 0.0, pltpu.roll(here, cz - 1, 1))
        if i > 0:
            near = near + fluid[i - 1]
        if i < cx - 1:
            near = near + fluid[i + 1]
        dry = liquid[i].astype(F32) * jnp.maximum(here - SATURATION, 0.0)
        base[i] = here + DIFFUSION * (near - 6.0 * here) - EVAPORATION * dry

    for load in loads[5:7]:
        load.wait()
    mask = [jnp.broadcast_to(pat[0, :, o:o + 1].astype(F32), (tiles, width)) for o in range(NB)]
    ones = jnp.ones((2 * width, width), BF16)
    eye = rows_of((width, width)) == lax.broadcasted_iota(jnp.int32, (width, width), 1)

    @pl.when(has_left)
    def _():
        pre_r_in = send(pre_out.at[1], pre_in.at[0], pre_send.at[1], pre_recv.at[0], {"gx": left})
        pre_r_in.wait_recv()

    @pl.when(has_right)
    def _():
        pre_l_in = send(pre_out.at[0], pre_in.at[1], pre_send.at[0], pre_recv.at[1], {"gx": right})
        pre_l_in.wait_recv()

    def own_ids(q):
        return dst[q, 0]

    def near_ids(side):
        return lambda q: pre_in[side, pl.ds(q, 1), :].astype(jnp.int32)

    for copy in arrivals:
        copy.wait_recv()

    def spread(run, ids_of):
        gather[run] = jnp.zeros((2 * tiles, width), F32)

        def add_group(c):
            lhs, rhs = [], []
            for j in range(group):
                q = c * group + j
                ids = ids_of(q)
                placed = jnp.where(rows_of((tiles, width)) == ids >> 7, arr[q, run], 0.0)
                high, low = split(placed)
                lhs.append(jnp.concatenate([high, low], axis=0))
                hit = rows_of((width, width)) == ids & (width - 1)
                rhs.append(jnp.where(hit, 1.0, 0.0).astype(BF16))
            gather[run] += dot_nt(jnp.concatenate(lhs, axis=1), jnp.concatenate(rhs, axis=1))

        repeat(chunks, add_group)
        both = gather[run]
        return both[0:tiles] + both[tiles:2 * tiles]

    right_side = fixed + spread(1, own_ids)
    iterate = inverse * right_side
    for side, run, lo, at in ((0, 0, tiles - REACH, 0), (1, 2, 0, tiles + REACH)):
        summed = spread(run, near_ids(side))[lo:lo + REACH]
        fixed_near = pre_in[side, senders:senders + REACH, :]
        inverse_near = pre_in[side, senders + REACH:senders + 2 * REACH, :]
        ext[at:at + REACH, :] = inverse_near * (fixed_near + summed)

    def windows():
        for o in range(NB):
            win[o] = mask[o] * ext[o:o + tiles, :]

    def couple(slot, pairs_of):
        for t, offsets in pairs_of:
            total = None
            for o in offsets:
                term = blocks[0, t, o] * win[o, t:t + 1, :]
                total = term if total is None else total + term
            high, low = split(total)
            summed = dot(jnp.concatenate([high, low], axis=1), ones)
            sums[slot, t:t + 1, :] = jnp.sum(jnp.where(eye, summed, 0.0), axis=0, keepdims=True)

    def inside(t, o):
        return 0 <= t + o - REACH < tiles

    every = [(t, list(range(NB))) for t in range(tiles)]
    local = [(t, [o for o in range(NB) if inside(t, o)]) for t in range(tiles)]
    outer = [(t, [o for o in range(NB) if not inside(t, o)]) for t in range(tiles)]
    outer = [(t, offsets) for t, offsets in outer if offsets]

    def pass_on(k):
        halo_out[k, 0] = iterate[0:REACH]
        halo_out[k, 1] = iterate[tiles - REACH:tiles]

        @pl.when(has_left)
        def _():
            halo_l[k].start()

        @pl.when(has_right)
        def _():
            halo_r[k].start()

    def take(k):
        @pl.when(has_left)
        def _():
            halo_r[k].wait_recv()

        @pl.when(has_right)
        def _():
            halo_l[k].wait_recv()

    ext[REACH:REACH + tiles, :] = iterate
    windows()
    couple(0, every)
    update = inverse * (right_side - diagonal * iterate - sums[0])
    iterate = iterate + update
    sums[1] = jnp.zeros((tiles, width), F32)
    rho_old = 0.5
    for k in range(SWEEPS - 1):
        pass_on(k)
        rho_next = 1.0 / (4.0 - rho_old)
        ext[...] = jnp.zeros_like(ext)
        ext[REACH:REACH + tiles, :] = iterate
        windows()
        couple(0, local)
        part = right_side - diagonal * iterate - sums[0]
        if k == 0:
            for face in faces:
                face.wait_recv()
            base[0] += DIFFUSION * x_in[0]
            base[cx - 1] += DIFFUSION * x_in[1]
            base[:, 0, :] += DIFFUSION * y_in[0]
            base[:, cy - 1, :] += DIFFUSION * y_in[1]
        if k == 1:
            deep = rows_of((cz, 128))
            for s in range(rows // 128):
                cut = slice(s * 128, (s + 1) * 128)
                layer = jnp.where(deep == 0, z_in[0, :, cut], 0.0)
                layer = layer + jnp.where(deep == cz - 1, z_in[1, :, cut], 0.0)
                base[s * per:(s + 1) * per] += DIFFUSION * layer.T.reshape(per, cy, cz)
        take(k)
        ext[0:REACH, :] = halo[k, 0]
        ext[tiles + REACH:tiles + 2 * REACH, :] = halo[k, 1]
        windows()
        couple(1, outer)
        residual = part - sums[1]
        update = rho_next * rho_old * update + 4.0 * rho_next * inverse * residual
        iterate = iterate + update
        rho_old = rho_next

    high, low = split(iterate)
    pair = jnp.concatenate([high, low], axis=0)

    def pick_back(c):
        rhs = []
        for j in range(group):
            hit = rows_of((width, width)) == dst[c * group + j, 0] & (width - 1)
            rhs.append(jnp.where(hit, 1.0, 0.0).astype(BF16))
        picked = dot(pair, jnp.concatenate(rhs, axis=1))
        picked = picked[0:tiles] + picked[tiles:2 * tiles]
        for j in range(group):
            row = dst[c * group + j, 0] >> 7
            part = jnp.where(rows_of((tiles, width)) == row, picked[:, j * width:(j + 1) * width], 0.0)
            sent[c * group + j] = jnp.sum(part, axis=0, keepdims=True)

    repeat(chunks, pick_back)
    backs = []
    for d in range(1, senders):
        peer = lax.rem(me + d, senders)
        backs.append(send(sent.at[peer], ret.at[me], ret_send.at[d], ret_recv.at[d], {"gx": peer}))
        backs[-1].start()
    ret[pl.ds(me, 1)] = sent[pl.ds(me, 1)]
    solid_ref[0] = iterate
    for copy in arrivals + faces:
        copy.wait_send()

    @pl.when(has_left)
    def _():
        for copy in [pre_l] + halo_l:
            copy.wait_send()

    @pl.when(has_right)
    def _():
        for copy in [pre_r] + halo_r:
            copy.wait_send()

    for copy in backs:
        copy.wait_recv()

    def spread_back(c):
        halves = []
        for j in range(group):
            q = c * group + j
            depth = src[q, 0] & (cz - 1)
            value = WALL_COUPLING * (ret[q] - outp[q + 1])
            placed = jnp.where(rows_of((cz, width)) == depth, value, 0.0)
            halves.append(jnp.concatenate(split(placed), axis=0))
        placed = jnp.concatenate(halves, axis=1)
        for s in range(0, rows, 256):
            both = dot_nt(hot[c, s:s + 256, :], placed)
            both = (both[:, 0:cz] + both[:, cz:2 * cz]).reshape(256 // cy, cy, cz)
            cut = slice(s // cy, (s + 256) // cy)
            if chunks == 1:
                new_ref[cut] = base[cut] + both
            else:
                base[cut] += both

    repeat(chunks, spread_back)
    if chunks > 1:
        new_ref[...] = base[...]
    for copy in backs:
        copy.wait_send()


def per_device(fluid_temp, liquid, face_src, face_dst, solid_old, solid_diag, blocks, pattern):
    senders = lax.axis_size("gx")
    group = 2 if senders % 2 == 0 else 1
    cx, cy, cz = fluid_temp.shape
    rows = cx * cy
    tiles, width = solid_old.shape[1:]
    pre_rows = (senders + 2 * REACH + 7) // 8 * 8
    ext_rows = (tiles + 2 * REACH + 7) // 8 * 8
    dma = pltpu.SemaphoreType.DMA
    args = (fluid_temp, liquid, face_src, face_dst, solid_old, solid_diag, blocks, pattern)
    scratch = [pltpu.VMEM(a.shape, a.dtype) for a in args]
    scratch += [
        pltpu.VMEM((senders // group, rows, group * width), BF16),
        pltpu.VMEM((2 * cz, rows), BF16),
        pltpu.VMEM((cx, cy, cz), F32),
        pltpu.VMEM((senders + 2, 1, width), F32),
        pltpu.VMEM((senders, 3, 1, width), F32),
        pltpu.VMEM((senders, 1, width), F32),
        pltpu.VMEM((senders, 1, width), F32),
        pltpu.VMEM((2, pre_rows, width), F32),
        pltpu.VMEM((2, pre_rows, width), F32),
        pltpu.VMEM((SWEEPS - 1, 2, REACH, width), F32),
        pltpu.VMEM((SWEEPS - 1, 2, REACH, width), F32),
        pltpu.VMEM((2, cy, cz), F32),
        pltpu.VMEM((2, cx, cz), F32),
        pltpu.VMEM((2, cx, cz), F32),
        pltpu.VMEM((2, 1, rows), F32),
        pltpu.VMEM((2, 1, rows), F32),
        pltpu.VMEM((ext_rows, width), F32),
        pltpu.VMEM((3, 2 * tiles, width), F32),
        pltpu.VMEM((NB, tiles, width), F32),
        pltpu.VMEM((2, tiles, width), F32),
        dma((8,)),
        dma((senders,)), dma((senders,)),
        dma((senders,)), dma((senders,)),
        dma((2,)), dma((2,)),
        dma((SWEEPS - 1, 2)), dma((SWEEPS - 1, 2)),
        dma((6,)), dma((6,)),
    ]
    return pl.pallas_call(
        functools.partial(kernel, senders, group),
        out_shape=(
            jax.ShapeDtypeStruct(fluid_temp.shape, F32),
            jax.ShapeDtypeStruct(solid_old.shape, F32),
        ),
        in_specs=[pl.BlockSpec(memory_space=pl.ANY)] * 8,
        out_specs=(pl.BlockSpec(memory_space=pltpu.VMEM),) * 2,
        scratch_shapes=scratch,
        compiler_params=pltpu.CompilerParams(
            collective_id=0, has_side_effects=True, vmem_limit_bytes=56 * 1024 * 1024
        ),
    )(*args)


def solution(mesh):
    return jax.shard_map(
        per_device,
        mesh=mesh,
        in_specs=(
            P("gx", "gy", "gz"),
            P("gx", "gy", "gz"),
            P("gx", "gy", "gz", None),
            P("gx", "gy", "gz", None),
            P(("gy", "gz"), "gx", None),
            P(("gy", "gz"), "gx", None),
            P(("gy", "gz"), "gx", None, None, None),
            P(("gy", "gz"), "gx", None),
        ),
        out_specs=(P("gx", "gy", "gz"), P(("gy", "gz"), "gx", None)),
        check_vma=False,
    )
```

time: 100 us -> 27.2 us (0.27); the launches traced: 98.4 us -> 26.9 us
  starting transfers between devices: 26.3 us -> 0 us
  Pallas kernels: 0 us -> 21.8 us
  waiting for transfers between devices: 18 us -> 0 us
  other arithmetic: 16.6 us -> 0 us
  matrix products: 16.2 us -> 0 us
  local copies, waits for them, and re-layouts: 20.4 us -> 4.5 us
    pallas_call x0 -> x1, Pallas kernels: none -> 21.8 us  [per_device(): pl.pallas_call(functools.partial(kernel, senders, group), out_shape=(jax....]
    ppermute x14 -> x0, starting transfers between devices: 18.8 us -> none  [the longest x7 11.3 us: padded_2(): after = lax.ppermute(leading, axis, down)]
    dot_general x8 -> x0, matrix products: 16.2 us -> none  [the longest x4 10.4 us: apply_tiles(): jnp.einsum('tjab,tjb->ta', blocks_run, neighbours, precision=lax.Precisio...]
    ppermute x14 -> x0, waiting for transfers between devices: 15.8 us -> none  [the longest x7 15.8 us: padded_2(): after = lax.ppermute(leading, axis, down)]
    add x5 -> x0, other arithmetic: 11.2 us -> none  [the longest x1 11.1 us: per_device(): fluid_temp + DIFFUSION * laplacian]
    all_to_all x2 -> x0, starting transfers between devices: 7.49 us -> none  [the longest x1 4.21 us: per_device(): lax.all_to_all(outgoing, 'gx', split_axis=0, concat_axis=0, tiled=True)]
    unnamed x24 -> x3, local copies, waits for them, and re-layouts: 11.7 us -> 4.5 us
    ppermute x2 -> x0, local copies, waits for them, and re-layouts: 3.34 us -> none  [the longest x1 1.69 us: padded_2(): before = lax.ppermute(last, axis, up)]
  transfers between devices with their start and end apart: 16 -> 0, of which waited for: 5 -> 0; matrix products, arithmetic and copies ran while one was open for 23% -> 0% of each run, Pallas kernels for 0% -> 0%
where the time goes in v1:
time: 27.2 us; the launch traced here: 26.9 us
  Pallas kernels  21.8 us (80%)
  local copies, waits for them, and re-layouts  4.5 us (17%)
  between operations  0.64 us (2%)
    pallas_call x1, Pallas kernels, per_device(): pl.pallas_call(functools.partial(kernel, senders, group), out_shape=(jax....  21.8 us
    unnamed x3, local copies, waits for them, and re-layouts  4.5 us

profile of v1, /device:TPU:0, one launch (start us, length us, event | category | flops | bytes accessed | tf_op | source)
XLA Modules:
  0.0 26.9 jit_solution(678062289096423582)
XLA Ops:
  0.6 1.4 %copy.10.pat_h = s32[1,8,5]{2,1,0:T(8,128)} copy(s32[1,8,5]{1,0,2:T(1,128)} %param.15) | data formatting | bytes 320 | tf_op args[7]
  2.0 21.8 %shard_map.95 = (f32[16,64,128]{2,1,0:T(8,128)}, f32[1,8,128]{2,1,0:T(8,128)}) custom-call(f32[16,64,128]{2,1,0:T(8,128)} %fluid_h.1, s32[16,64,128]{2,1,0:T(8,128)} %liquid_h.1, s32[2,1,1,128]{3,2,1,0:T(1,128)} %src_h.1, s32[2,1,1,128]{3,2,1,0:T(1,128)} %dst_h.1, f32[1,8,128]{2,1,0:T(8,128)} %old_h.1, f32[1,8,128]{2,1,0:T(8,128)} %diag_h.1, ...), custom_call_target="tpu_custom_call" | custom-call | tf_op jit(solution)/shard_map/pallas_call | solution.py:432
  23.8 1.9 %copy.13 = f32[16,64,128]{2,1,0:T(8,128)} copy(f32[16,64,128]{2,1,0:T(8,128)} %get-tuple-element.4) | data formatting | bytes 1048576
  25.7 1.3 %copy.14 = f32[1,8,128]{2,1,0:T(8,128)} copy(f32[1,8,128]{2,1,0:T(8,128)} %get-tuple-element.5) | data formatting | bytes 8192

commit v2 on v1

v2 whole, which is shorter than its diff:
```python
import functools

import jax
import jax.numpy as jnp
from jax import lax
from jax.experimental import pallas as pl
from jax.experimental.pallas import tpu as pltpu
from jax.sharding import PartitionSpec as P

REACH = 2
SWEEPS = 4
NB = 5
DIFFUSION = 0.12
EVAPORATION = 0.5
SATURATION = 0.25
WALL_COUPLING = 0.2
MESH = pl.DeviceIdType.MESH
F32 = jnp.float32
BF16 = jnp.bfloat16


def split(values):
    high = values.astype(BF16)
    return high, (values - high.astype(F32)).astype(BF16)


def dot(a, b):
    return jnp.dot(a, b, preferred_element_type=F32)


def dot_nt(a, b):
    return lax.dot_general(a, b, (((1,), (1,)), ((), ())), preferred_element_type=F32)


def rows_of(shape):
    return lax.broadcasted_iota(jnp.int32, shape, 0)


def repeat(count, body):
    if count == 1:
        body(0)
    else:
        pl.loop(0, count)(body)


def kernel(
    senders, group,
    fluid_h, liquid_h, src_h, dst_h, old_h, diag_h, blocks_h, pat_h,
    base, hot, src, wall, solid,
    fluid, liquid, dst, old, diag, blocks, pat,
    spot, table, outp, arr, sent, ret, pre_out, pre_in, halo_out, halo,
    x_in, y_out, y_in, z_out, z_in, ext, gather, sums,
    load_sem, arr_send, arr_recv, ret_send, ret_recv, pre_send, pre_recv,
    halo_send, halo_recv, face_send, face_recv, go, cross,
):
    cx, cy, cz = fluid.shape
    rows = cx * cy
    tiles, width = old.shape[1], old.shape[2]
    chunks = senders // group
    me = lax.axis_index("gx")
    gy, gz = lax.axis_index("gy"), lax.axis_index("gz")
    ny, nz = lax.axis_size("gy"), lax.axis_size("gz")
    left, right = lax.rem(me + senders - 1, senders), lax.rem(me + 1, senders)
    below, above = lax.rem(gy + ny - 1, ny), lax.rem(gy + 1, ny)
    before, after = lax.rem(gz + nz - 1, nz), lax.rem(gz + 1, nz)
    has_left, has_right = me > 0, me < senders - 1
    late = lax.rem(gz, 2) == 1
    barrier = pltpu.get_barrier_semaphore()

    @pl.when(me != 0)
    def _():
        pl.semaphore_signal(barrier, inc=1, device_id={"gx": 0}, device_id_type=MESH)

    pairs = [(src_h, src), (fluid_h, fluid), (dst_h, dst), (old_h, old), (diag_h, diag),
             (pat_h, pat), (blocks_h, blocks), (liquid_h, liquid)]
    loads = [pltpu.make_async_copy(a, b, load_sem.at[i]) for i, (a, b) in enumerate(pairs)]
    for load in loads:
        load.start()

    def send(source, target, send_sem, recv_sem, device):
        return pltpu.make_async_remote_copy(
            src_ref=source, dst_ref=target, send_sem=send_sem, recv_sem=recv_sem,
            device_id=device, device_id_type=MESH)

    outp[...] = jnp.zeros_like(outp)
    ext[...] = jnp.zeros_like(ext)
    sums[...] = jnp.zeros_like(sums)
    loads[0].wait()

    def make_hot(c):
        for j in range(group):
            row = src[c * group + j, 0] >> 7
            for s in range(0, rows, 128):
                hit = rows_of((128, width)) + s == row
                hot[c, s:s + 128, j * width:(j + 1) * width] = jnp.where(hit, 1.0, 0.0).astype(BF16)

    repeat(chunks, make_hot)

    @pl.when(me == 0)
    def _():
        pl.semaphore_wait(barrier, senders - 1)
        for d in range(1, senders):
            pl.semaphore_signal(go, inc=1, device_id={"gx": d}, device_id_type=MESH)

    for load in loads[2:5]:
        load.wait()
    diagonal = diag[0]
    inverse = 1.0 / diagonal
    fixed = diagonal * old[0]
    for side, lo in ((0, 0), (1, tiles - REACH)):
        for q in range(senders):
            pre_out[side, q:q + 1, :] = dst[q, 0].astype(F32)
        pre_out[side, senders:senders + REACH, :] = fixed[lo:lo + REACH]
        pre_out[side, senders + REACH:senders + 2 * REACH, :] = inverse[lo:lo + REACH]

    loads[1].wait()
    per = 128 // cy
    for s in range(rows // 128):
        flipped = fluid[s * per:(s + 1) * per].reshape(128, cz).T
        high, low = split(flipped)
        table[0:cz, s * 128:(s + 1) * 128] = high
        table[cz:2 * cz, s * 128:(s + 1) * 128] = low
        z_out[0, :, s * 128:(s + 1) * 128] = flipped[0:1]
        z_out[1, :, s * 128:(s + 1) * 128] = flipped[cz - 1:cz]

    def pick(c):
        picked = dot(table[...], hot[c])
        picked = picked[0:cz] + picked[cz:2 * cz]
        for j in range(group):
            depth = src[c * group + j, 0] & (cz - 1)
            part = picked[:, j * width:(j + 1) * width]
            part = jnp.where(rows_of((cz, width)) == depth, part, 0.0)
            outp[c * group + j + 1] = jnp.sum(part, axis=0, keepdims=True)

    repeat(chunks, pick)

    @pl.when(me != 0)
    def _():
        pl.semaphore_wait(go, 1)

    @pl.when(me == 1)
    def _():
        for peer in ({"gy": below}, {"gy": above}, {"gz": before}, {"gz": after}):
            pl.semaphore_signal(barrier, inc=1, device_id=peer, device_id_type=MESH)

    pre_l = send(pre_out.at[0], pre_in.at[1], pre_send.at[0], pre_recv.at[1], {"gx": left})
    pre_r = send(pre_out.at[1], pre_in.at[0], pre_send.at[1], pre_recv.at[0], {"gx": right})
    halo_l = [send(halo_out.at[k, 0], halo.at[k, 1], halo_send.at[k, 0], halo_recv.at[k, 1],
                   {"gx": left}) for k in range(SWEEPS - 1)]
    halo_r = [send(halo_out.at[k, 1], halo.at[k, 0], halo_send.at[k, 1], halo_recv.at[k, 0],
                   {"gx": right}) for k in range(SWEEPS - 1)]
    arrivals = []
    for d in range(1, senders):
        peer = lax.rem(me + d, senders)
        arrivals.append(send(outp.at[pl.ds(peer, 3)], arr.at[me], arr_send.at[d], arr_recv.at[d],
                             {"gx": peer}))

    @pl.when(has_left)
    def _():
        pre_l.start()

    @pl.when(has_right)
    def _():
        pre_r.start()

    for copy in arrivals:
        copy.start()
    faces = [
        send(fluid.at[0], x_in.at[1], face_send.at[0], face_recv.at[0], {"gx": left}),
        send(fluid.at[cx - 1], x_in.at[0], face_send.at[1], face_recv.at[1], {"gx": right}),
        send(y_out.at[0], y_in.at[1], face_send.at[2], face_recv.at[2], {"gy": below}),
        send(y_out.at[1], y_in.at[0], face_send.at[3], face_recv.at[3], {"gy": above}),
        send(z_out.at[0], z_in.at[1], face_send.at[4], face_recv.at[4], {"gz": before}),
        send(z_out.at[1], z_in.at[0], face_send.at[5], face_recv.at[5], {"gz": after}),
    ]
    for face in faces[0:2]:
        face.start()
    arr[pl.ds(me, 1)] = outp[pl.ds(me, 3)][None]
    y_out[0] = fluid[:, 0, :]
    y_out[1] = fluid[:, cy - 1, :]

    @pl.when(jnp.logical_not(has_left))
    def _():
        pre_in[0] = jnp.zeros_like(pre_in[0])
        for k in range(SWEEPS - 1):
            halo[k, 0] = jnp.zeros_like(halo[k, 0])

    @pl.when(jnp.logical_not(has_right))
    def _():
        pre_in[1] = jnp.zeros_like(pre_in[1])
        for k in range(SWEEPS - 1):
            halo[k, 1] = jnp.zeros_like(halo[k, 1])

    for load in loads[5:7]:
        load.wait()
    small = rows_of((tiles, tiles)) == lax.broadcasted_iota(jnp.int32, (tiles, tiles), 1)
    for o in range(NB):
        row = jnp.broadcast_to(pat[o].astype(F32), (tiles, tiles))
        column = jnp.sum(jnp.where(small, row, 0.0), axis=1, keepdims=True)
        mask = jnp.broadcast_to(column, (tiles, width))
        for t in range(tiles):
            blocks[0, t, o] = blocks[0, t, o] * mask[t:t + 1]

    @pl.when(has_left)
    def _():
        send(pre_out.at[1], pre_in.at[0], pre_send.at[1], pre_recv.at[0], {"gx": left}).wait_recv()

    @pl.when(has_right)
    def _():
        send(pre_out.at[0], pre_in.at[1], pre_send.at[0], pre_recv.at[1], {"gx": right}).wait_recv()

    def ids_at(run, q):
        if run == 1:
            return dst[q, 0]
        return pre_in[run // 2, pl.ds(q, 1), :].astype(jnp.int32)

    def make_spot(c):
        for run in range(3):
            for j in range(group):
                hit = rows_of((width, width)) == ids_at(run, c * group + j) & (width - 1)
                spot[run, c, :, j * width:(j + 1) * width] = jnp.where(hit, 1.0, 0.0).astype(BF16)

    repeat(chunks, make_spot)
    ones = jnp.ones((2 * width, width), BF16)
    eye = rows_of((width, width)) == lax.broadcasted_iota(jnp.int32, (width, width), 1)
    for copy in arrivals:
        copy.wait_recv()

    gather[...] = jnp.zeros_like(gather)

    def add_group(c):
        for run in range(3):
            lhs = []
            for j in range(group):
                q = c * group + j
                hit = rows_of((tiles, width)) == ids_at(run, q) >> 7
                high, low = split(jnp.where(hit, arr[q, run], 0.0))
                lhs.append(jnp.concatenate([high, low], axis=0))
            gather[run] += dot_nt(jnp.concatenate(lhs, axis=1), spot[run, c])

    repeat(chunks, add_group)
    gathered = [gather[run, 0:tiles] + gather[run, tiles:2 * tiles] for run in range(3)]
    right_side = fixed + gathered[1]
    iterate = inverse * right_side
    ext[REACH:REACH + tiles, :] = iterate
    for side, run, lo, at in ((0, 0, tiles - REACH, 0), (1, 2, 0, tiles + REACH)):
        fixed_near = pre_in[side, senders:senders + REACH, :]
        inverse_near = pre_in[side, senders + REACH:senders + 2 * REACH, :]
        ext[at:at + REACH, :] = inverse_near * (fixed_near + gathered[run][lo:lo + REACH])

    def couple(slot, pairs_of):
        for t, offsets in pairs_of:
            total = None
            for o in offsets:
                term = blocks[0, t, o] * ext[t + o:t + o + 1, :]
                total = term if total is None else total + term
            high, low = split(total)
            summed = dot(jnp.concatenate([high, low], axis=1), ones)
            sums[slot, t:t + 1, :] = jnp.sum(jnp.where(eye, summed, 0.0), axis=0, keepdims=True)

    def inside(t, o):
        return 0 <= t + o - REACH < tiles

    every = list(range(NB))
    edge = [(t, every) for t in range(tiles) if t < REACH or t >= tiles - REACH]
    middle = [(t, every) for t in range(tiles) if REACH <= t < tiles - REACH]
    local = [(t, [o for o in every if inside(t, o)]) for t in range(tiles)]
    outer = [(t, [o for o in every if not inside(t, o)]) for t in range(tiles)]
    outer = [(t, offsets) for t, offsets in outer if offsets]

    def pass_on(k, values):
        halo_out[k, 0] = values[0:REACH]
        halo_out[k, 1] = values[tiles - REACH:tiles]

        @pl.when(has_left)
        def _():
            halo_l[k].start()

        @pl.when(has_right)
        def _():
            halo_r[k].start()

    def take(k):
        @pl.when(has_left)
        def _():
            halo_r[k].wait_recv()

        @pl.when(has_right)
        def _():
            halo_l[k].wait_recv()

    def meet_first(turn):
        @pl.when(jnp.logical_and(turn, me == 1))
        def _():
            pl.semaphore_wait(barrier, 4)
            for d in range(1, senders):
                pl.semaphore_signal(cross, inc=1, device_id={"gx": lax.rem(me + d, senders)},
                                    device_id_type=MESH)
            for face in faces[2:]:
                face.start()

    def meet_rest(turn):
        @pl.when(jnp.logical_and(turn, me != 1))
        def _():
            pl.semaphore_wait(cross, 1)
            for face in faces[2:]:
                face.start()

    lane = lax.broadcasted_iota(jnp.int32, (cy, cz), 1)
    line = lax.broadcasted_iota(jnp.int32, (cy, cz), 0)

    def stencil(first, last):
        for i in range(first, last):
            here = fluid[i]
            near = jnp.where(line == 0, 0.0, pltpu.roll(here, 1, 0))
            near = near + jnp.where(line == cy - 1, 0.0, pltpu.roll(here, cy - 1, 0))
            near = near + jnp.where(lane == 0, 0.0, pltpu.roll(here, 1, 1))
            near = near + jnp.where(lane == cz - 1, 0.0, pltpu.roll(here, cz - 1, 1))
            if i > 0:
                near = near + fluid[i - 1]
            if i < cx - 1:
                near = near + fluid[i + 1]
            dry = liquid[i].astype(F32) * jnp.maximum(here - SATURATION, 0.0)
            base[i] = here + DIFFUSION * (near - 6.0 * here) - EVAPORATION * dry

    couple(0, edge)
    pass_on(0, iterate + inverse * (right_side - diagonal * iterate - sums[0]))
    couple(0, middle)
    update = inverse * (right_side - diagonal * iterate - sums[0])
    iterate = iterate + update
    rho_old = 0.5
    for k in range(SWEEPS - 1):
        if k > 0:
            pass_on(k, iterate)
        if k == 0:
            meet_first(late)
        if k == SWEEPS - 2:
            meet_first(jnp.logical_not(late))
        rho_next = 1.0 / (4.0 - rho_old)
        ext[REACH:REACH + tiles, :] = iterate
        couple(0, local)
        part = right_side - diagonal * iterate - sums[0]
        if k == 0:
            loads[7].wait()
            stencil(0, cx // 2)
            meet_rest(late)
        if k == 1:
            stencil(cx // 2, cx)
        if k == SWEEPS - 2:
            for face in faces[0:2]:
                face.wait_recv()
            base[0] += DIFFUSION * x_in[0]
            base[cx - 1] += DIFFUSION * x_in[1]
            meet_rest(jnp.logical_not(late))
        take(k)
        ext[0:REACH, :] = halo[k, 0]
        ext[tiles + REACH:tiles + 2 * REACH, :] = halo[k, 1]
        couple(1, outer)
        residual = part - sums[1]
        update = rho_next * rho_old * update + 4.0 * rho_next * inverse * residual
        iterate = iterate + update
        rho_old = rho_next

    high, low = split(iterate)
    both = jnp.concatenate([high, low], axis=0)

    def pick_back(c):
        picked = dot(both, spot[1, c])
        picked = picked[0:tiles] + picked[tiles:2 * tiles]
        for j in range(group):
            row = dst[c * group + j, 0] >> 7
            part = jnp.where(rows_of((tiles, width)) == row, picked[:, j * width:(j + 1) * width], 0.0)
            sent[c * group + j] = jnp.sum(part, axis=0, keepdims=True)

    repeat(chunks, pick_back)
    backs = []
    for d in range(1, senders):
        peer = lax.rem(me + d, senders)
        backs.append(send(sent.at[peer], ret.at[me], ret_send.at[d], ret_recv.at[d], {"gx": peer}))
        backs[-1].start()
    ret[pl.ds(me, 1)] = sent[pl.ds(me, 1)]
    solid[0] = iterate

    for face in faces[2:]:
        face.wait_recv()
    base[:, 0, :] += DIFFUSION * y_in[0]
    base[:, cy - 1, :] += DIFFUSION * y_in[1]
    deep = rows_of((cz, 128))
    for s in range(rows // 128):
        cut = slice(s * 128, (s + 1) * 128)
        layer = jnp.where(deep == 0, z_in[0, :, cut], 0.0)
        layer = layer + jnp.where(deep == cz - 1, z_in[1, :, cut], 0.0)
        base[s * per:(s + 1) * per] += DIFFUSION * layer.T.reshape(per, cy, cz)

    for copy in arrivals + faces:
        copy.wait_send()

    @pl.when(has_left)
    def _():
        for copy in [pre_l] + halo_l:
            copy.wait_send()

    @pl.when(has_right)
    def _():
        for copy in [pre_r] + halo_r:
            copy.wait_send()

    for copy in backs:
        copy.wait()
    wall[...] = WALL_COUPLING * (ret[...] - outp[1:senders + 1])


def finish(group, base, hot, src, wall, solid, new_h, solid_h, new, sems):
    cx, cy, cz = base.shape
    rows = cx * cy
    chunks, width = hot.shape[0], src.shape[-1]
    solid_copy = pltpu.make_async_copy(solid, solid_h, sems.at[0])
    solid_copy.start()

    def placed_of(c):
        halves = []
        for j in range(group):
            q = c * group + j
            placed = jnp.where(rows_of((cz, width)) == src[q, 0] & (cz - 1), wall[q], 0.0)
            halves.append(jnp.concatenate(split(placed), axis=0))
        return jnp.concatenate(halves, axis=1)

    step = rows // 4
    cuts = [slice(s * step // cy, (s + 1) * step // cy) for s in range(4)]

    def added(c, s, placed):
        both = dot_nt(hot[c, s * step:(s + 1) * step, :], placed)
        return (both[:, 0:cz] + both[:, cz:2 * cz]).reshape(step // cy, cy, cz)

    if chunks > 1:
        def add_chunk(c):
            placed = placed_of(c)
            for s in range(4):
                base_now = jnp.where(c == 0, base[cuts[s]], new[cuts[s]])
                new[cuts[s]] = base_now + added(c, s, placed)

        pl.loop(0, chunks)(add_chunk)
    else:
        placed = placed_of(0)
    copies = []
    for s in range(4):
        if chunks == 1:
            new[cuts[s]] = base[cuts[s]] + added(0, s, placed)
        copies.append(pltpu.make_async_copy(new.at[cuts[s]], new_h.at[cuts[s]], sems.at[s + 1]))
        copies[-1].start()
    for copy in [solid_copy] + copies:
        copy.wait()


def per_device(fluid_temp, liquid, face_src, face_dst, solid_old, solid_diag, blocks, pattern):
    senders = lax.axis_size("gx")
    group = 2 if senders % 2 == 0 else 1
    chunks = senders // group
    cx, cy, cz = fluid_temp.shape
    rows = cx * cy
    tiles, width = solid_old.shape[1:]
    pre_rows = (senders + 2 * REACH + 7) // 8 * 8
    ext_rows = (tiles + 2 * REACH + 7) // 8 * 8
    dma = pltpu.SemaphoreType.DMA
    pattern = jnp.transpose(pattern, (2, 0, 1))
    args = (fluid_temp, liquid, face_src, face_dst, solid_old, solid_diag, blocks, pattern)
    args = tuple(pltpu.with_memory_space_constraint(a, pltpu.HBM) for a in args)
    scratch = [pltpu.VMEM(a.shape, a.dtype)
               for a in (fluid_temp, liquid, face_dst, solid_old, solid_diag, blocks, pattern)]
    scratch += [
        pltpu.VMEM((3, chunks, width, group * width), BF16),
        pltpu.VMEM((2 * cz, rows), BF16),
        pltpu.VMEM((senders + 2, 1, width), F32),
        pltpu.VMEM((senders, 3, 1, width), F32),
        pltpu.VMEM((senders, 1, width), F32),
        pltpu.VMEM((senders, 1, width), F32),
        pltpu.VMEM((2, pre_rows, width), F32),
        pltpu.VMEM((2, pre_rows, width), F32),
        pltpu.VMEM((SWEEPS - 1, 2, REACH, width), F32),
        pltpu.VMEM((SWEEPS - 1, 2, REACH, width), F32),
        pltpu.VMEM((2, cy, cz), F32),
        pltpu.VMEM((2, cx, cz), F32),
        pltpu.VMEM((2, cx, cz), F32),
        pltpu.VMEM((2, 1, rows), F32),
        pltpu.VMEM((2, 1, rows), F32),
        pltpu.VMEM((ext_rows, width), F32),
        pltpu.VMEM((3, 2 * tiles, width), F32),
        pltpu.VMEM((2, tiles, width), F32),
        dma((8,)),
        dma((senders,)), dma((senders,)),
        dma((senders,)), dma((senders,)),
        dma((2,)), dma((2,)),
        dma((SWEEPS - 1, 2)), dma((SWEEPS - 1, 2)),
        dma((6,)), dma((6,)),
        pltpu.SemaphoreType.REGULAR, pltpu.SemaphoreType.REGULAR,
    ]
    parts = pl.pallas_call(
        functools.partial(kernel, senders, group),
        out_shape=(
            pltpu.VMEM(fluid_temp.shape, F32),
            pltpu.VMEM((chunks, rows, group * width), BF16),
            pltpu.VMEM(face_src.shape, jnp.int32),
            pltpu.VMEM((senders, 1, width), F32),
            pltpu.VMEM(solid_old.shape, F32),
        ),
        in_specs=[pl.BlockSpec(memory_space=pltpu.HBM)] * 8,
        out_specs=(pl.BlockSpec(memory_space=pltpu.VMEM),) * 5,
        scratch_shapes=scratch,
        compiler_params=pltpu.CompilerParams(
            collective_id=0, has_side_effects=True, vmem_limit_bytes=24 * 1024 * 1024
        ),
    )(*args)
    parts = tuple(pltpu.with_memory_space_constraint(p, pltpu.VMEM) for p in parts)
    return pl.pallas_call(
        functools.partial(finish, group),
        out_shape=(
            jax.ShapeDtypeStruct(fluid_temp.shape, F32),
            jax.ShapeDtypeStruct(solid_old.shape, F32),
        ),
        in_specs=[pl.BlockSpec(memory_space=pltpu.VMEM)] * 5,
        out_specs=(pl.BlockSpec(memory_space=pl.ANY),) * 2,
        scratch_shapes=[pltpu.VMEM(fluid_temp.shape, F32), dma((5,))],
        compiler_params=pltpu.CompilerParams(vmem_limit_bytes=16 * 1024 * 1024),
    )(*parts)


def solution(mesh):
    return jax.shard_map(
        per_device,
        mesh=mesh,
        in_specs=(
            P("gx", "gy", "gz"),
            P("gx", "gy", "gz"),
            P("gx", "gy", "gz", None),
            P("gx", "gy", "gz", None),
            P(("gy", "gz"), "gx", None),
            P(("gy", "gz"), "gx", None),
            P(("gy", "gz"), "gx", None, None, None),
            P(("gy", "gz"), "gx", None),
        ),
        out_specs=(P("gx", "gy", "gz"), P(("gy", "gz"), "gx", None)),
        check_vma=False,
    )
```

time: 27.2 us -> 21.1 us (0.78)
  local copies, waits for them, and re-layouts: 4.5 us -> 0 us
  Pallas kernels: 21.8 us -> 20.3 us
    unnamed x3 -> x0, local copies, waits for them, and re-layouts: 4.5 us -> none
    pallas_call x1 -> x2, Pallas kernels: 21.8 us -> 20.3 us  [the longest x1 19.2 us: per_device(): pl.pallas_call(functools.partial(kernel, senders, group), out_shape=(pltp...]
where the time goes in v2:
time: 21.1 us; the launch traced here: 20.9 us
  Pallas kernels  20.3 us (96%)
  between operations  0.64 us (3%)
    pallas_call x1, Pallas kernels, per_device(): pl.pallas_call(functools.partial(kernel, senders, group), out_shape=(pltp...  19.2 us
    pallas_call x1, Pallas kernels, per_device(): pl.pallas_call(functools.partial(finish, group), out_shape=(jax.ShapeDtyp...  1.1 us

profile of v2, /device:TPU:0, one launch (start us, length us, event | category | flops | bytes accessed | tf_op | source)
XLA Modules:
  0.0 20.9 jit_solution(1964819734375631695)
XLA Ops:
  0.6 19.2 %shard_map.95 = (f32[16,64,128]{2,1,0:T(8,128)S(1)}, bf16[1,1024,256]{2,1,0:T(8,128)(2,1)S(1)}, s32[2,1,1,128]{3,2,1,0:T(1,128)S(1)}, f32[2,1,128]{2,1,0:T(1,128)S(1)}, f32[1,8,128]{2,1,0:T(8,128)S(1)}) custom-call(f32[16,64,128]{2,1,0:T(8,128)} %fluid_h.1, s32[16,64,128]{2,1,0:T(8,128)} %liquid_h.1, s32[2,1,1,128]{3,2,1,0:T(1,128)} %src_h.1, ...), custom_call_target="tpu_custom_call" | custom-call | tf_op jit(solution)/shard_map/pallas_call | solution.py:497
  19.8 1.1 %shard_map.96 = (f32[16,64,128]{2,1,0:T(8,128)}, f32[1,8,128]{2,1,0:T(8,128)}) custom-call(f32[16,64,128]{2,1,0:T(8,128)S(1)} %get-tuple-element.7.base, bf16[1,1024,256]{2,1,0:T(8,128)(2,1)S(1)} %get-tuple-element.8.hot, s32[2,1,1,128]{3,2,1,0:T(1,128)S(1)} %get-tuple-element.9.src, f32[2,1,128]{2,1,0:T(1,128)S(1)} %get-tuple-element.10.wall, ...), custom_call_target="tpu_custom_call" | custom-call | tf_op jit(solution)/shard_map/pallas_call | solution.py:514

commit v3 on v2

--- a/solution.py
+++ b/solution.py
@@ -51,7 +51,7 @@
     spot, table, outp, arr, sent, ret, pre_out, pre_in, halo_out, halo,
     x_in, y_out, y_in, z_out, z_in, ext, gather, sums,
     load_sem, arr_send, arr_recv, ret_send, ret_recv, pre_send, pre_recv,
-    halo_send, halo_recv, face_send, face_recv, go, cross,
+    halo_send, halo_recv, face_send, face_recv, go, cross, near,
 ):
     cx, cy, cz = fluid.shape
     rows = cx * cy
@@ -65,11 +65,27 @@
     before, after = lax.rem(gz + nz - 1, nz), lax.rem(gz + 1, nz)
     has_left, has_right = me > 0, me < senders - 1
     late = lax.rem(gz, 2) == 1
+    early = jnp.logical_not(late)
     barrier = pltpu.get_barrier_semaphore()
 
-    @pl.when(me != 0)
-    def _():
-        pl.semaphore_signal(barrier, inc=1, device_id={"gx": 0}, device_id_type=MESH)
+    def signal(semaphore, device):
+        pl.semaphore_signal(semaphore, inc=1, device_id=device, device_id_type=MESH)
+
+    @pl.when(late)
+    def _():
+        for d in range(1, senders):
+            signal(barrier, {"gx": lax.rem(me + d, senders)})
+        signal(barrier, {"gy": below})
+        signal(barrier, {"gy": above})
+
+    @pl.when(early)
+    def _():
+        signal(barrier, {"gz": before})
+        signal(barrier, {"gz": after})
+
+    @pl.when(jnp.logical_and(early, me != 0))
+    def _():
+        signal(barrier, {"gx": 0})
 
     pairs = [(src_h, src), (fluid_h, fluid), (dst_h, dst), (old_h, old), (diag_h, diag),
              (pat_h, pat), (blocks_h, blocks), (liquid_h, liquid)]
@@ -96,11 +112,11 @@
 
     repeat(chunks, make_hot)
 
-    @pl.when(me == 0)
+    @pl.when(jnp.logical_and(early, me == 0))
     def _():
         pl.semaphore_wait(barrier, senders - 1)
         for d in range(1, senders):
-            pl.semaphore_signal(go, inc=1, device_id={"gx": d}, device_id_type=MESH)
+            signal(go, {"gx": d})
 
     for load in loads[2:5]:
         load.wait()
@@ -134,14 +150,20 @@
 
     repeat(chunks, pick)
 
-    @pl.when(me != 0)
+    @pl.when(late)
+    def _():
+        pl.semaphore_wait(barrier, senders + 3)
+        signal(near, {"gz": before})
+        signal(near, {"gz": after})
+
+    @pl.when(jnp.logical_and(early, me != 0))
     def _():
         pl.semaphore_wait(go, 1)
 
-    @pl.when(me == 1)
-    def _():
-        for peer in ({"gy": below}, {"gy": above}, {"gz": before}, {"gz": after}):
-            pl.semaphore_signal(barrier, inc=1, device_id=peer, device_id_type=MESH)
+    @pl.when(jnp.logical_and(early, me == 1))
+    def _():
+        signal(barrier, {"gy": below})
+        signal(barrier, {"gy": above})
 
     pre_l = send(pre_out.at[0], pre_in.at[1], pre_send.at[0], pre_recv.at[1], {"gx": left})
     pre_r = send(pre_out.at[1], pre_in.at[0], pre_send.at[1], pre_recv.at[0], {"gx": right})
@@ -165,6 +187,8 @@
 
     for copy in arrivals:
         copy.start()
+    y_out[0] = fluid[:, 0, :]
+    y_out[1] = fluid[:, cy - 1, :]
     faces = [
         send(fluid.at[0], x_in.at[1], face_send.at[0], face_recv.at[0], {"gx": left}),
         send(fluid.at[cx - 1], x_in.at[0], face_send.at[1], face_recv.at[1], {"gx": right}),
@@ -173,11 +197,15 @@
         send(z_out.at[0], z_in.at[1], face_send.at[4], face_recv.at[4], {"gz": before}),
         send(z_out.at[1], z_in.at[0], face_send.at[5], face_recv.at[5], {"gz": after}),
     ]
+
+    @pl.when(late)
+    def _():
+        for face in faces[2:]:
+            face.start()
+
     for face in faces[0:2]:
         face.start()
     arr[pl.ds(me, 1)] = outp[pl.ds(me, 3)][None]
-    y_out[0] = fluid[:, 0, :]
-    y_out[1] = fluid[:, cy - 1, :]
 
     @pl.when(jnp.logical_not(has_left))
     def _():
@@ -289,21 +317,20 @@
         def _():
             halo_l[k].wait_recv()
 
-    def meet_first(turn):
-        @pl.when(jnp.logical_and(turn, me == 1))
+    def meet_first():
+        @pl.when(jnp.logical_and(early, me == 1))
         def _():
-            pl.semaphore_wait(barrier, 4)
+            pl.semaphore_wait(barrier, 2)
             for d in range(1, senders):
-                pl.semaphore_signal(cross, inc=1, device_id={"gx": lax.rem(me + d, senders)},
-                                    device_id_type=MESH)
-            for face in faces[2:]:
+                signal(cross, {"gx": lax.rem(me + d, senders)})
+            for face in faces[2:4]:
                 face.start()
 
-    def meet_rest(turn):
-        @pl.when(jnp.logical_and(turn, me != 1))
+    def meet_rest():
+        @pl.when(jnp.logical_and(early, me != 1))
         def _():
             pl.semaphore_wait(cross, 1)
-            for face in faces[2:]:
+            for face in faces[2:4]:
                 face.start()
 
     lane = lax.broadcasted_iota(jnp.int32, (cy, cz), 1)
@@ -332,10 +359,8 @@
     for k in range(SWEEPS - 1):
         if k > 0:
             pass_on(k, iterate)
-        if k == 0:
-            meet_first(late)
-        if k == SWEEPS - 2:
-            meet_first(jnp.logical_not(late))
+        if k == 1:
+            meet_first()
         rho_next = 1.0 / (4.0 - rho_old)
         ext[REACH:REACH + tiles, :] = iterate
         couple(0, local)
@@ -343,15 +368,14 @@
         if k == 0:
             loads[7].wait()
             stencil(0, cx // 2)
-            meet_rest(late)
         if k == 1:
             stencil(cx // 2, cx)
+            meet_rest()
         if k == SWEEPS - 2:
             for face in faces[0:2]:
                 face.wait_recv()
             base[0] += DIFFUSION * x_in[0]
             base[cx - 1] += DIFFUSION * x_in[1]
-            meet_rest(jnp.logical_not(late))
         take(k)
         ext[0:REACH, :] = halo[k, 0]
         ext[tiles + REACH:tiles + 2 * REACH, :] = halo[k, 1]
@@ -378,6 +402,13 @@
         peer = lax.rem(me + d, senders)
         backs.append(send(sent.at[peer], ret.at[me], ret_send.at[d], ret_recv.at[d], {"gx": peer}))
         backs[-1].start()
+
+    @pl.when(early)
+    def _():
+        pl.semaphore_wait(near, 2)
+        for face in faces[4:]:
+            face.start()
+
     ret[pl.ds(me, 1)] = sent[pl.ds(me, 1)]
     solid[0] = iterate
 
@@ -492,7 +523,7 @@
         dma((2,)), dma((2,)),
         dma((SWEEPS - 1, 2)), dma((SWEEPS - 1, 2)),
         dma((6,)), dma((6,)),
-        pltpu.SemaphoreType.REGULAR, pltpu.SemaphoreType.REGULAR,
+        pltpu.SemaphoreType.REGULAR, pltpu.SemaphoreType.REGULAR, pltpu.SemaphoreType.REGULAR,
     ]
     parts = pl.pallas_call(
         functools.partial(kernel, senders, group),

time: 21.1 us -> 20.5 us (0.972)
  Pallas kernels: 20.3 us -> 19.7 us
    pallas_call x1, Pallas kernels: 19.2 us -> 18.6 us  [per_device(): pl.pallas_call(functools.partial(kernel, senders, group), out_shape=(pltp...]
where the time goes in v3:
time: 20.5 us; the launch traced here: 20.3 us
  Pallas kernels  19.7 us (96%)
  between operations  0.64 us (3%)
    pallas_call x1, Pallas kernels, per_device(): pl.pallas_call(functools.partial(kernel, senders, group), out_shape=(pltp...  18.6 us
    pallas_call x1, Pallas kernels, per_device(): pl.pallas_call(functools.partial(finish, group), out_shape=(jax.ShapeDtyp...  1.1 us

profile of v3, /device:TPU:0, one launch (start us, length us, event | category | flops | bytes accessed | tf_op | source)
XLA Modules:
  0.0 20.3 jit_solution(2659238815705552)
XLA Ops:
  0.6 18.6 %shard_map.95 = (f32[16,64,128]{2,1,0:T(8,128)S(1)}, bf16[1,1024,256]{2,1,0:T(8,128)(2,1)S(1)}, s32[2,1,1,128]{3,2,1,0:T(1,128)S(1)}, f32[2,1,128]{2,1,0:T(1,128)S(1)}, f32[1,8,128]{2,1,0:T(8,128)S(1)}) custom-call(f32[16,64,128]{2,1,0:T(8,128)} %fluid_h.1, s32[16,64,128]{2,1,0:T(8,128)} %liquid_h.1, s32[2,1,1,128]{3,2,1,0:T(1,128)} %src_h.1, ...), custom_call_target="tpu_custom_call" | custom-call | tf_op jit(solution)/shard_map/pallas_call | solution.py:528
  19.2 1.1 %shard_map.96 = (f32[16,64,128]{2,1,0:T(8,128)}, f32[1,8,128]{2,1,0:T(8,128)}) custom-call(f32[16,64,128]{2,1,0:T(8,128)S(1)} %get-tuple-element.7.base, bf16[1,1024,256]{2,1,0:T(8,128)(2,1)S(1)} %get-tuple-element.8.hot, s32[2,1,1,128]{3,2,1,0:T(1,128)S(1)} %get-tuple-element.9.src, f32[2,1,128]{2,1,0:T(1,128)S(1)} %get-tuple-element.10.wall, ...), custom_call_target="tpu_custom_call" | custom-call | tf_op jit(solution)/shard_map/pallas_call | solution.py:545

commit v4 on v2

--- a/solution.py
+++ b/solution.py
@@ -48,10 +48,10 @@
     fluid_h, liquid_h, src_h, dst_h, old_h, diag_h, blocks_h, pat_h,
     base, hot, src, wall, solid,
     fluid, liquid, dst, old, diag, blocks, pat,
-    spot, table, outp, arr, sent, ret, pre_out, pre_in, halo_out, halo,
+    spot, back, table, outp, arr, sent, ret, pre_out, pre_in, halo_out, halo,
     x_in, y_out, y_in, z_out, z_in, ext, gather, sums,
     load_sem, arr_send, arr_recv, ret_send, ret_recv, pre_send, pre_recv,
-    halo_send, halo_recv, face_send, face_recv, go, cross,
+    halo_send, halo_recv, face_send, face_recv,
 ):
     cx, cy, cz = fluid.shape
     rows = cx * cy
@@ -64,12 +64,12 @@
     below, above = lax.rem(gy + ny - 1, ny), lax.rem(gy + 1, ny)
     before, after = lax.rem(gz + nz - 1, nz), lax.rem(gz + 1, nz)
     has_left, has_right = me > 0, me < senders - 1
-    late = lax.rem(gz, 2) == 1
     barrier = pltpu.get_barrier_semaphore()
 
-    @pl.when(me != 0)
-    def _():
-        pl.semaphore_signal(barrier, inc=1, device_id={"gx": 0}, device_id_type=MESH)
+    peers = [{"gx": lax.rem(me + d, senders)} for d in range(1, senders)]
+    peers += [{"gy": below}, {"gy": above}, {"gz": before}, {"gz": after}]
+    for peer in peers:
+        pl.semaphore_signal(barrier, inc=1, device_id=peer, device_id_type=MESH)
 
     pairs = [(src_h, src), (fluid_h, fluid), (dst_h, dst), (old_h, old), (diag_h, diag),
              (pat_h, pat), (blocks_h, blocks), (liquid_h, liquid)]
@@ -95,12 +95,6 @@
                 hot[c, s:s + 128, j * width:(j + 1) * width] = jnp.where(hit, 1.0, 0.0).astype(BF16)
 
     repeat(chunks, make_hot)
-
-    @pl.when(me == 0)
-    def _():
-        pl.semaphore_wait(barrier, senders - 1)
-        for d in range(1, senders):
-            pl.semaphore_signal(go, inc=1, device_id={"gx": d}, device_id_type=MESH)
 
     for load in loads[2:5]:
         load.wait()
@@ -134,14 +128,7 @@
 
     repeat(chunks, pick)
 
-    @pl.when(me != 0)
-    def _():
-        pl.semaphore_wait(go, 1)
-
-    @pl.when(me == 1)
-    def _():
-        for peer in ({"gy": below}, {"gy": above}, {"gz": before}, {"gz": after}):
-            pl.semaphore_signal(barrier, inc=1, device_id=peer, device_id_type=MESH)
+    pl.semaphore_wait(barrier, len(peers))
 
     pre_l = send(pre_out.at[0], pre_in.at[1], pre_send.at[0], pre_recv.at[1], {"gx": left})
     pre_r = send(pre_out.at[1], pre_in.at[0], pre_send.at[1], pre_recv.at[0], {"gx": right})
@@ -165,6 +152,8 @@
 
     for copy in arrivals:
         copy.start()
+    y_out[0] = fluid[:, 0, :]
+    y_out[1] = fluid[:, cy - 1, :]
     faces = [
         send(fluid.at[0], x_in.at[1], face_send.at[0], face_recv.at[0], {"gx": left}),
         send(fluid.at[cx - 1], x_in.at[0], face_send.at[1], face_recv.at[1], {"gx": right}),
@@ -173,23 +162,17 @@
         send(z_out.at[0], z_in.at[1], face_send.at[4], face_recv.at[4], {"gz": before}),
         send(z_out.at[1], z_in.at[0], face_send.at[5], face_recv.at[5], {"gz": after}),
     ]
-    for face in faces[0:2]:
+    for face in faces:
         face.start()
     arr[pl.ds(me, 1)] = outp[pl.ds(me, 3)][None]
-    y_out[0] = fluid[:, 0, :]
-    y_out[1] = fluid[:, cy - 1, :]
 
     @pl.when(jnp.logical_not(has_left))
     def _():
         pre_in[0] = jnp.zeros_like(pre_in[0])
-        for k in range(SWEEPS - 1):
-            halo[k, 0] = jnp.zeros_like(halo[k, 0])
 
     @pl.when(jnp.logical_not(has_right))
     def _():
         pre_in[1] = jnp.zeros_like(pre_in[1])
-        for k in range(SWEEPS - 1):
-            halo[k, 1] = jnp.zeros_like(halo[k, 1])
 
     for load in loads[5:7]:
         load.wait()
@@ -218,7 +201,10 @@
         for run in range(3):
             for j in range(group):
                 hit = rows_of((width, width)) == ids_at(run, c * group + j) & (width - 1)
-                spot[run, c, :, j * width:(j + 1) * width] = jnp.where(hit, 1.0, 0.0).astype(BF16)
+                hit = jnp.where(hit, 1.0, 0.0)
+                back[run, c, j * width:(j + 1) * width, :] = hit.T.astype(BF16)
+                if run == 1:
+                    spot[c, :, j * width:(j + 1) * width] = hit.astype(BF16)
 
     repeat(chunks, make_spot)
     ones = jnp.ones((2 * width, width), BF16)
@@ -236,7 +222,7 @@
                 hit = rows_of((tiles, width)) == ids_at(run, q) >> 7
                 high, low = split(jnp.where(hit, arr[q, run], 0.0))
                 lhs.append(jnp.concatenate([high, low], axis=0))
-            gather[run] += dot_nt(jnp.concatenate(lhs, axis=1), spot[run, c])
+            gather[run] += dot(jnp.concatenate(lhs, axis=1), back[run, c])
 
     repeat(chunks, add_group)
     gathered = [gather[run, 0:tiles] + gather[run, tiles:2 * tiles] for run in range(3)]
@@ -262,49 +248,37 @@
         return 0 <= t + o - REACH < tiles
 
     every = list(range(NB))
-    edge = [(t, every) for t in range(tiles) if t < REACH or t >= tiles - REACH]
-    middle = [(t, every) for t in range(tiles) if REACH <= t < tiles - REACH]
+    middle = [(t, every) for t in range(REACH, tiles - REACH)]
     local = [(t, [o for o in every if inside(t, o)]) for t in range(tiles)]
-    outer = [(t, [o for o in every if not inside(t, o)]) for t in range(tiles)]
-    outer = [(t, offsets) for t, offsets in outer if offsets]
+    first = [(t, every) for t in range(REACH)]
+    last = [(t, every) for t in range(tiles - REACH, tiles)]
+    outer_first = [(t, [o for o in every if t + o < REACH]) for t in range(REACH)]
+    outer_last = [(t, [o for o in every if t + o >= tiles + REACH]) for t in range(tiles - REACH, tiles)]
+    no_left, no_right = jnp.logical_not(has_left), jnp.logical_not(has_right)
 
     def pass_on(k, values):
-        halo_out[k, 0] = values[0:REACH]
-        halo_out[k, 1] = values[tiles - REACH:tiles]
-
         @pl.when(has_left)
         def _():
+            halo_out[k, 0] = values[0:REACH]
             halo_l[k].start()
 
         @pl.when(has_right)
         def _():
+            halo_out[k, 1] = values[tiles - REACH:tiles]
             halo_r[k].start()
 
     def take(k):
         @pl.when(has_left)
         def _():
             halo_r[k].wait_recv()
+            ext[0:REACH, :] = halo[k, 0]
+            couple(1, outer_first)
 
         @pl.when(has_right)
         def _():
             halo_l[k].wait_recv()
-
-    def meet_first(turn):
-        @pl.when(jnp.logical_and(turn, me == 1))
-        def _():
-            pl.semaphore_wait(barrier, 4)
-            for d in range(1, senders):
-                pl.semaphore_signal(cross, inc=1, device_id={"gx": lax.rem(me + d, senders)},
-                                    device_id_type=MESH)
-            for face in faces[2:]:
-                face.start()
-
-    def meet_rest(turn):
-        @pl.when(jnp.logical_and(turn, me != 1))
-        def _():
-            pl.semaphore_wait(cross, 1)
-            for face in faces[2:]:
-                face.start()
+            ext[tiles + REACH:tiles + 2 * REACH, :] = halo[k, 1]
+            couple(1, outer_last)
 
     lane = lax.broadcasted_iota(jnp.int32, (cy, cz), 1)
     line = lax.broadcasted_iota(jnp.int32, (cy, cz), 0)
@@ -323,8 +297,31 @@
             dry = liquid[i].astype(F32) * jnp.maximum(here - SATURATION, 0.0)
             base[i] = here + DIFFUSION * (near - 6.0 * here) - EVAPORATION * dry
 
-    couple(0, edge)
-    pass_on(0, iterate + inverse * (right_side - diagonal * iterate - sums[0]))
+    def step(lo):
+        cut = slice(lo, lo + REACH)
+        rest = right_side[cut] - diagonal[cut] * iterate[cut] - sums[0, cut, :]
+        return iterate[cut] + inverse[cut] * rest
+
+    @pl.when(has_left)
+    def _():
+        couple(0, first)
+        halo_out[0, 0] = step(0)
+        halo_l[0].start()
+
+    @pl.when(has_right)
+    def _():
+        couple(0, last)
+        halo_out[0, 1] = step(tiles - REACH)
+        halo_r[0].start()
+
+    @pl.when(no_left)
+    def _():
+        couple(0, first)
+
+    @pl.when(no_right)
+    def _():
+        couple(0, last)
+
     couple(0, middle)
     update = inverse * (right_side - diagonal * iterate - sums[0])
     iterate = iterate + update
@@ -332,10 +329,6 @@
     for k in range(SWEEPS - 1):
         if k > 0:
             pass_on(k, iterate)
-        if k == 0:
-            meet_first(late)
-        if k == SWEEPS - 2:
-            meet_first(jnp.logical_not(late))
         rho_next = 1.0 / (4.0 - rho_old)
         ext[REACH:REACH + tiles, :] = iterate
         couple(0, local)
@@ -343,7 +336,6 @@
         if k == 0:
             loads[7].wait()
             stencil(0, cx // 2)
-            meet_rest(late)
         if k == 1:
             stencil(cx // 2, cx)
         if k == SWEEPS - 2:
@@ -351,11 +343,7 @@
                 face.wait_recv()
             base[0] += DIFFUSION * x_in[0]
             base[cx - 1] += DIFFUSION * x_in[1]
-            meet_rest(jnp.logical_not(late))
         take(k)
-        ext[0:REACH, :] = halo[k, 0]
-        ext[tiles + REACH:tiles + 2 * REACH, :] = halo[k, 1]
-        couple(1, outer)
         residual = part - sums[1]
         update = rho_next * rho_old * update + 4.0 * rho_next * inverse * residual
         iterate = iterate + update
@@ -365,7 +353,7 @@
     both = jnp.concatenate([high, low], axis=0)
 
     def pick_back(c):
-        picked = dot(both, spot[1, c])
+        picked = dot(both, spot[c])
         picked = picked[0:tiles] + picked[tiles:2 * tiles]
         for j in range(group):
             row = dst[c * group + j, 0] >> 7
@@ -468,7 +456,8 @@
     scratch = [pltpu.VMEM(a.shape, a.dtype)
                for a in (fluid_temp, liquid, face_dst, solid_old, solid_diag, blocks, pattern)]
     scratch += [
-        pltpu.VMEM((3, chunks, width, group * width), BF16),
+        pltpu.VMEM((chunks, width, group * width), BF16),
+        pltpu.VMEM((3, chunks, group * width, width), BF16),
         pltpu.VMEM((2 * cz, rows), BF16),
         pltpu.VMEM((senders + 2, 1, width), F32),
         pltpu.VMEM((senders, 3, 1, width), F32),
@@ -492,7 +481,6 @@
         dma((2,)), dma((2,)),
         dma((SWEEPS - 1, 2)), dma((SWEEPS - 1, 2)),
         dma((6,)), dma((6,)),
-        pltpu.SemaphoreType.REGULAR, pltpu.SemaphoreType.REGULAR,
     ]
     parts = pl.pallas_call(
         functools.partial(kernel, senders, group),

time: 21.1 us -> 21.9 us (1.038)
  Pallas kernels: 20.3 us -> 21.1 us
    pallas_call x1, Pallas kernels: 19.2 us -> 20 us  [per_device(): pl.pallas_call(functools.partial(kernel, senders, group), out_shape=(pltp...]
where the time goes in v4:
time: 21.9 us; the launch traced here: 21.7 us
  Pallas kernels  21.1 us (96%)
  between operations  0.64 us (3%)
    pallas_call x1, Pallas kernels, per_device(): pl.pallas_call(functools.partial(kernel, senders, group), out_shape=(pltp...  20 us
    pallas_call x1, Pallas kernels, per_device(): pl.pallas_call(functools.partial(finish, group), out_shape=(jax.ShapeDtyp...  1.1 us

profile of v4, /device:TPU:0, one launch (start us, length us, event | category | flops | bytes accessed | tf_op | source)
XLA Modules:
  0.0 21.7 jit_solution(17145936297918166029)
XLA Ops:
  0.6 20.0 %shard_map.95 = (f32[16,64,128]{2,1,0:T(8,128)S(1)}, bf16[1,1024,256]{2,1,0:T(8,128)(2,1)S(1)}, s32[2,1,1,128]{3,2,1,0:T(1,128)S(1)}, f32[2,1,128]{2,1,0:T(1,128)S(1)}, f32[1,8,128]{2,1,0:T(8,128)S(1)}) custom-call(f32[16,64,128]{2,1,0:T(8,128)} %fluid_h.1, s32[16,64,128]{2,1,0:T(8,128)} %liquid_h.1, s32[2,1,1,128]{3,2,1,0:T(1,128)} %src_h.1, ...), custom_call_target="tpu_custom_call" | custom-call | tf_op jit(solution)/shard_map/pallas_call | solution.py:485
  20.6 1.1 %shard_map.96 = (f32[16,64,128]{2,1,0:T(8,128)}, f32[1,8,128]{2,1,0:T(8,128)}) custom-call(f32[16,64,128]{2,1,0:T(8,128)S(1)} %get-tuple-element.7.base, bf16[1,1024,256]{2,1,0:T(8,128)(2,1)S(1)} %get-tuple-element.8.hot, s32[2,1,1,128]{3,2,1,0:T(1,128)S(1)} %get-tuple-element.9.src, f32[2,1,128]{2,1,0:T(1,128)S(1)} %get-tuple-element.10.wall, ...), custom_call_target="tpu_custom_call" | custom-call | tf_op jit(solution)/shard_map/pallas_call | solution.py:502

commit v5 on v4

--- a/solution.py
+++ b/solution.py
@@ -49,9 +49,9 @@
     base, hot, src, wall, solid,
     fluid, liquid, dst, old, diag, blocks, pat,
     spot, back, table, outp, arr, sent, ret, pre_out, pre_in, halo_out, halo,
-    x_in, y_out, y_in, z_out, z_in, ext, gather, sums,
+    x_in, y_out, y_in, z_out, z_in, ext, gather, sums, edge,
     load_sem, arr_send, arr_recv, ret_send, ret_recv, pre_send, pre_recv,
-    halo_send, halo_recv, face_send, face_recv,
+    halo_send, halo_recv, face_send, face_recv, near_sem,
 ):
     cx, cy, cz = fluid.shape
     rows = cx * cy
@@ -66,10 +66,21 @@
     has_left, has_right = me > 0, me < senders - 1
     barrier = pltpu.get_barrier_semaphore()
 
-    peers = [{"gx": lax.rem(me + d, senders)} for d in range(1, senders)]
-    peers += [{"gy": below}, {"gy": above}, {"gz": before}, {"gz": after}]
-    for peer in peers:
-        pl.semaphore_signal(barrier, inc=1, device_id=peer, device_id_type=MESH)
+    line_peers = [{"gx": lax.rem(me + d, senders)} for d in range(1, senders)]
+    cross_peers = [{"gy": below}, {"gy": above}, {"gz": before}, {"gz": after}]
+    odd = lax.rem(gy + gz, 2) == 1
+    even = jnp.logical_not(odd)
+
+    def signal(semaphore, device):
+        pl.semaphore_signal(semaphore, inc=1, device_id=device, device_id_type=MESH)
+
+    for peer in line_peers:
+        signal(barrier, peer)
+
+    @pl.when(even)
+    def _():
+        for peer in cross_peers:
+            signal(barrier, peer)
 
     pairs = [(src_h, src), (fluid_h, fluid), (dst_h, dst), (old_h, old), (diag_h, diag),
              (pat_h, pat), (blocks_h, blocks), (liquid_h, liquid)]
@@ -128,7 +139,7 @@
 
     repeat(chunks, pick)
 
-    pl.semaphore_wait(barrier, len(peers))
+    pl.semaphore_wait(barrier, jnp.where(odd, len(line_peers) + len(cross_peers), len(line_peers)))
 
     pre_l = send(pre_out.at[0], pre_in.at[1], pre_send.at[0], pre_recv.at[1], {"gx": left})
     pre_r = send(pre_out.at[1], pre_in.at[0], pre_send.at[1], pre_recv.at[0], {"gx": right})
@@ -162,7 +173,15 @@
         send(z_out.at[0], z_in.at[1], face_send.at[4], face_recv.at[4], {"gz": before}),
         send(z_out.at[1], z_in.at[0], face_send.at[5], face_recv.at[5], {"gz": after}),
     ]
-    for face in faces:
+
+    @pl.when(odd)
+    def _():
+        for peer in cross_peers:
+            signal(near_sem, peer)
+        for face in faces[2:]:
+            face.start()
+
+    for face in faces[0:2]:
         face.start()
     arr[pl.ds(me, 1)] = outp[pl.ds(me, 3)][None]
 
@@ -252,33 +271,44 @@
     local = [(t, [o for o in every if inside(t, o)]) for t in range(tiles)]
     first = [(t, every) for t in range(REACH)]
     last = [(t, every) for t in range(tiles - REACH, tiles)]
-    outer_first = [(t, [o for o in every if t + o < REACH]) for t in range(REACH)]
-    outer_last = [(t, [o for o in every if t + o >= tiles + REACH]) for t in range(tiles - REACH, tiles)]
     no_left, no_right = jnp.logical_not(has_left), jnp.logical_not(has_right)
 
-    def pass_on(k, values):
-        @pl.when(has_left)
-        def _():
-            halo_out[k, 0] = values[0:REACH]
-            halo_l[k].start()
-
-        @pl.when(has_right)
-        def _():
-            halo_out[k, 1] = values[tiles - REACH:tiles]
-            halo_r[k].start()
-
-    def take(k):
-        @pl.when(has_left)
-        def _():
-            halo_r[k].wait_recv()
-            ext[0:REACH, :] = halo[k, 0]
-            couple(1, outer_first)
-
-        @pl.when(has_right)
-        def _():
-            halo_l[k].wait_recv()
-            ext[tiles + REACH:tiles + 2 * REACH, :] = halo[k, 1]
-            couple(1, outer_last)
+    sides = ((0, has_left, 0, 0, halo_r, halo_l),
+             (1, has_right, tiles - REACH, tiles + REACH, halo_l, halo_r))
+
+    def make_edges():
+        for side, has, lo, at, _, _ in sides:
+            @pl.when(has)
+            def _():
+                for i in range(REACH):
+                    for j in range(REACH):
+                        o = at + i - lo - j
+                        block = jnp.zeros((width, width), F32)
+                        if 0 <= o < NB:
+                            block = blocks[0, lo + j, o].T
+                        for part, values in enumerate(split(block)):
+                            column = (part * REACH + j) * width
+                            edge[side, i * width:(i + 1) * width, column:column + width] = values
+
+    def take(k, part, scale_old, scale_new):
+        for side, has, lo, _, copy_in, copy_out in sides:
+            @pl.when(has)
+            def _():
+                copy_in[k].wait_recv()
+                flat = jnp.concatenate([halo[k, side, i:i + 1, :] for i in range(REACH)], axis=1)
+                high = flat.astype(BF16).astype(F32)
+                lhs = [jnp.broadcast_to(v, (8, REACH * width)) for v in (high, flat - high)]
+                product = dot(jnp.concatenate(lhs, axis=0).astype(BF16), edge[side])
+                product = product[0:1] + product[8:9]
+                product = product[:, 0:REACH * width] + product[:, REACH * width:]
+                summed = [product[:, j * width:(j + 1) * width] for j in range(REACH)]
+                summed = jnp.concatenate(summed, axis=0)
+                cut = slice(lo, lo + REACH)
+                if k + 1 < SWEEPS - 1:
+                    change = scale_old * update[cut] + scale_new * inverse[cut] * (part[cut] - summed)
+                    halo_out[k + 1, side] = iterate[cut] + change
+                    copy_out[k + 1].start()
+                sums[1, cut, :] = summed
 
     lane = lax.broadcasted_iota(jnp.int32, (cy, cz), 1)
     line = lax.broadcasted_iota(jnp.int32, (cy, cz), 0)
@@ -327,8 +357,6 @@
     iterate = iterate + update
     rho_old = 0.5
     for k in range(SWEEPS - 1):
-        if k > 0:
-            pass_on(k, iterate)
         rho_next = 1.0 / (4.0 - rho_old)
         ext[REACH:REACH + tiles, :] = iterate
         couple(0, local)
@@ -338,12 +366,21 @@
             stencil(0, cx // 2)
         if k == 1:
             stencil(cx // 2, cx)
+
+            @pl.when(even)
+            def _():
+                pl.semaphore_wait(near_sem, len(cross_peers))
+                for face in faces[2:]:
+                    face.start()
+
         if k == SWEEPS - 2:
             for face in faces[0:2]:
                 face.wait_recv()
             base[0] += DIFFUSION * x_in[0]
             base[cx - 1] += DIFFUSION * x_in[1]
-        take(k)
+        if k == 0:
+            make_edges()
+        take(k, part, rho_next * rho_old, 4.0 * rho_next)
         residual = part - sums[1]
         update = rho_next * rho_old * update + 4.0 * rho_next * inverse * residual
         iterate = iterate + update
@@ -475,12 +512,14 @@
         pltpu.VMEM((ext_rows, width), F32),
         pltpu.VMEM((3, 2 * tiles, width), F32),
         pltpu.VMEM((2, tiles, width), F32),
+        pltpu.VMEM((2, REACH * width, 2 * REACH * width), BF16),
         dma((8,)),
         dma((senders,)), dma((senders,)),
         dma((senders,)), dma((senders,)),
         dma((2,)), dma((2,)),
         dma((SWEEPS - 1, 2)), dma((SWEEPS - 1, 2)),
         dma((6,)), dma((6,)),
+        pltpu.SemaphoreType.REGULAR,
     ]
     parts = pl.pallas_call(
         functools.partial(kernel, senders, group),

time: 21.9 us -> 19.7 us (0.90)
  Pallas kernels: 21.1 us -> 18.9 us
    pallas_call x1, Pallas kernels: 20 us -> 17.8 us  [per_device(): pl.pallas_call(functools.partial(kernel, senders, group), out_shape=(pltp...]
where the time goes in v5:
time: 19.7 us; the launch traced here: 19.5 us
  Pallas kernels  18.9 us (96%)
  between operations  0.64 us (3%)
    pallas_call x1, Pallas kernels, per_device(): pl.pallas_call(functools.partial(kernel, senders, group), out_shape=(pltp...  17.8 us
    pallas_call x1, Pallas kernels, per_device(): pl.pallas_call(functools.partial(finish, group), out_shape=(jax.ShapeDtyp...  1.09 us

profile of v5, /device:TPU:0, one launch (start us, length us, event | category | flops | bytes accessed | tf_op | source)
XLA Modules:
  0.0 19.5 jit_solution(12708924545838721698)
XLA Ops:
  0.6 17.8 %shard_map.95 = (f32[16,64,128]{2,1,0:T(8,128)S(1)}, bf16[1,1024,256]{2,1,0:T(8,128)(2,1)S(1)}, s32[2,1,1,128]{3,2,1,0:T(1,128)S(1)}, f32[2,1,128]{2,1,0:T(1,128)S(1)}, f32[1,8,128]{2,1,0:T(8,128)S(1)}) custom-call(f32[16,64,128]{2,1,0:T(8,128)} %fluid_h.1, s32[16,64,128]{2,1,0:T(8,128)} %liquid_h.1, s32[2,1,1,128]{3,2,1,0:T(1,128)} %src_h.1, ...), custom_call_target="tpu_custom_call" | custom-call | tf_op jit(solution)/shard_map/pallas_call | solution.py:524
  18.5 1.1 %shard_map.96 = (f32[16,64,128]{2,1,0:T(8,128)}, f32[1,8,128]{2,1,0:T(8,128)}) custom-call(f32[16,64,128]{2,1,0:T(8,128)S(1)} %get-tuple-element.7.base, bf16[1,1024,256]{2,1,0:T(8,128)(2,1)S(1)} %get-tuple-element.8.hot, s32[2,1,1,128]{3,2,1,0:T(1,128)S(1)} %get-tuple-element.9.src, f32[2,1,128]{2,1,0:T(1,128)S(1)} %get-tuple-element.10.wall, ...), custom_call_target="tpu_custom_call" | custom-call | tf_op jit(solution)/shard_map/pallas_call | solution.py:541

commit v6 on v5

--- a/solution.py
+++ b/solution.py
@@ -49,9 +49,9 @@
     base, hot, src, wall, solid,
     fluid, liquid, dst, old, diag, blocks, pat,
     spot, back, table, outp, arr, sent, ret, pre_out, pre_in, halo_out, halo,
-    x_in, y_out, y_in, z_out, z_in, ext, gather, sums, edge,
+    x_in, y_out, y_in, z_out, z_in, ext, gather, sums, edge, far_in, far_edge, own,
     load_sem, arr_send, arr_recv, ret_send, ret_recv, pre_send, pre_recv,
-    halo_send, halo_recv, face_send, face_recv, near_sem,
+    halo_send, halo_recv, face_send, face_recv, near_sem, far_send, far_recv,
 ):
     cx, cy, cz = fluid.shape
     rows = cx * cy
@@ -290,19 +290,63 @@
                             column = (part * REACH + j) * width
                             edge[side, i * width:(i + 1) * width, column:column + width] = values
 
+    def times_edge(values, matrix):
+        flat = jnp.concatenate([values[i:i + 1] for i in range(REACH)], axis=1)
+        high = flat.astype(BF16).astype(F32)
+        lhs = [jnp.broadcast_to(v, (8, REACH * width)) for v in (high, flat - high)]
+        product = dot(jnp.concatenate(lhs, axis=0).astype(BF16), matrix)
+        product = product[0:1] + product[8:9]
+        product = product[:, 0:REACH * width] + product[:, REACH * width:]
+        return jnp.concatenate([product[:, j * width:(j + 1) * width] for j in range(REACH)], axis=0)
+
+    merged = senders == 2
+    places = [(i, j) for i in range(REACH) for j in range(REACH)]
+
+    def far_blocks(side):
+        _, _, lo, at, _, _ = sides[side]
+        found = [(n, i, j, at + i - lo - j) for n, (i, j) in enumerate(places)]
+        return [entry for entry in found if 0 <= entry[3] < NB]
+
+    def far_copies(side):
+        lo = sides[side][2]
+        return [send(blocks.at[0, lo + j, o], far_in.at[n], far_send.at[n], far_recv.at[n],
+                     {"gx": left if side == 0 else right}) for n, i, j, o in far_blocks(side)]
+
+    def send_far():
+        for side, has, _, _, _, _ in sides:
+            @pl.when(has)
+            def _():
+                for copy in far_copies(side):
+                    copy.start()
+
+    def correct(scale_new):
+        for side, has, lo, _, _, _ in sides:
+            @pl.when(has)
+            def _():
+                for copy in far_copies(1 - side):
+                    copy.wait_recv()
+                far_edge[...] = jnp.zeros_like(far_edge)
+                for n, i, j, _ in far_blocks(1 - side):
+                    for half, values in enumerate(split(far_in[n].T)):
+                        column = (half * REACH + j) * width
+                        far_edge[i * width:(i + 1) * width, column:column + width] = values
+                summed = times_edge(iterate[lo:lo + REACH], far_edge[...])
+                change = -scale_new * pre_in[side, senders + REACH:senders + 2 * REACH, :] * summed
+                ids = pre_in[side, pl.ds(me, 1), :].astype(jnp.int32)
+                hit = rows_of((width, width)) == ids & (width - 1)
+                change = jnp.concatenate([change, jnp.zeros((8 - REACH, width), F32)], axis=0)
+                picked = dot(jnp.concatenate(split(change), axis=0), jnp.where(hit, 1.0, 0.0).astype(BF16))
+                picked = picked[0:8] + picked[8:16]
+                row = (ids >> 7) - (0 if side == 1 else tiles - REACH)
+                live = jnp.logical_and(rows_of((8, width)) == row, rows_of((8, width)) < REACH)
+                sums[0, 0:1, :] = jnp.sum(jnp.where(live, picked, 0.0), axis=0, keepdims=True)
+
     def take(k, part, scale_old, scale_new):
         for side, has, lo, _, copy_in, copy_out in sides:
             @pl.when(has)
             def _():
                 copy_in[k].wait_recv()
-                flat = jnp.concatenate([halo[k, side, i:i + 1, :] for i in range(REACH)], axis=1)
-                high = flat.astype(BF16).astype(F32)
-                lhs = [jnp.broadcast_to(v, (8, REACH * width)) for v in (high, flat - high)]
-                product = dot(jnp.concatenate(lhs, axis=0).astype(BF16), edge[side])
-                product = product[0:1] + product[8:9]
-                product = product[:, 0:REACH * width] + product[:, REACH * width:]
-                summed = [product[:, j * width:(j + 1) * width] for j in range(REACH)]
-                summed = jnp.concatenate(summed, axis=0)
+                summed = times_edge(halo[k, side], edge[side])
                 cut = slice(lo, lo + REACH)
                 if k + 1 < SWEEPS - 1:
                     change = scale_old * update[cut] + scale_new * inverse[cut] * (part[cut] - summed)
@@ -327,6 +371,37 @@
             dry = liquid[i].astype(F32) * jnp.maximum(here - SATURATION, 0.0)
             base[i] = here + DIFFUSION * (near - 6.0 * here) - EVAPORATION * dry
 
+    def finish_faces():
+        for face in faces[2:]:
+            face.wait_recv()
+        base[:, 0, :] += DIFFUSION * y_in[0]
+        base[:, cy - 1, :] += DIFFUSION * y_in[1]
+        deep = rows_of((cz, 128))
+        for s in range(rows // 128):
+            cut = slice(s * 128, (s + 1) * 128)
+            layer = jnp.where(deep == 0, z_in[0, :, cut], 0.0)
+            layer = layer + jnp.where(deep == cz - 1, z_in[1, :, cut], 0.0)
+            base[s * per:(s + 1) * per] += DIFFUSION * layer.T.reshape(per, cy, cz)
+
+    def pick_back(values, target):
+        both = jnp.concatenate(split(values), axis=0)
+
+        def pick_chunk(c):
+            picked = dot(both, spot[c])
+            picked = picked[0:tiles] + picked[tiles:2 * tiles]
+            for j in range(group):
+                row = dst[c * group + j, 0] >> 7
+                part = picked[:, j * width:(j + 1) * width]
+                part = jnp.where(rows_of((tiles, width)) == row, part, 0.0)
+                target[c * group + j] = jnp.sum(part, axis=0, keepdims=True)
+
+        repeat(chunks, pick_chunk)
+
+    backs = []
+    for d in range(1, senders):
+        peer = lax.rem(me + d, senders)
+        backs.append(send(sent.at[peer], ret.at[me], ret_send.at[d], ret_recv.at[d], {"gx": peer}))
+
     def step(lo):
         cut = slice(lo, lo + REACH)
         rest = right_side[cut] - diagonal[cut] * iterate[cut] - sums[0, cut, :]
@@ -359,13 +434,13 @@
     for k in range(SWEEPS - 1):
         rho_next = 1.0 / (4.0 - rho_old)
         ext[REACH:REACH + tiles, :] = iterate
+        if merged and k == 1:
+            send_far()
         couple(0, local)
         part = right_side - diagonal * iterate - sums[0]
         if k == 0:
             loads[7].wait()
             stencil(0, cx // 2)
-        if k == 1:
-            stencil(cx // 2, cx)
 
             @pl.when(even)
             def _():
@@ -373,11 +448,21 @@
                 for face in faces[2:]:
                     face.start()
 
+        if k == 1:
+            stencil(cx // 2, cx)
+        if merged and k == SWEEPS - 2:
+            change = rho_next * rho_old * update + 4.0 * rho_next * inverse * part
+            pick_back(iterate + change, sent)
+            for copy in backs:
+                copy.start()
+            correct(4.0 * rho_next)
         if k == SWEEPS - 2:
             for face in faces[0:2]:
                 face.wait_recv()
             base[0] += DIFFUSION * x_in[0]
             base[cx - 1] += DIFFUSION * x_in[1]
+            if merged:
+                finish_faces()
         if k == 0:
             make_edges()
         take(k, part, rho_next * rho_old, 4.0 * rho_next)
@@ -386,36 +471,17 @@
         iterate = iterate + update
         rho_old = rho_next
 
-    high, low = split(iterate)
-    both = jnp.concatenate([high, low], axis=0)
-
-    def pick_back(c):
-        picked = dot(both, spot[c])
-        picked = picked[0:tiles] + picked[tiles:2 * tiles]
-        for j in range(group):
-            row = dst[c * group + j, 0] >> 7
-            part = jnp.where(rows_of((tiles, width)) == row, picked[:, j * width:(j + 1) * width], 0.0)
-            sent[c * group + j] = jnp.sum(part, axis=0, keepdims=True)
-
-    repeat(chunks, pick_back)
-    backs = []
-    for d in range(1, senders):
-        peer = lax.rem(me + d, senders)
-        backs.append(send(sent.at[peer], ret.at[me], ret_send.at[d], ret_recv.at[d], {"gx": peer}))
-        backs[-1].start()
-    ret[pl.ds(me, 1)] = sent[pl.ds(me, 1)]
+    if merged:
+        pick_back(iterate, own)
+        ret[pl.ds(me, 1)] = own[pl.ds(me, 1)]
+    else:
+        pick_back(iterate, sent)
+        for copy in backs:
+            copy.start()
+        ret[pl.ds(me, 1)] = sent[pl.ds(me, 1)]
     solid[0] = iterate
-
-    for face in faces[2:]:
-        face.wait_recv()
-    base[:, 0, :] += DIFFUSION * y_in[0]
-    base[:, cy - 1, :] += DIFFUSION * y_in[1]
-    deep = rows_of((cz, 128))
-    for s in range(rows // 128):
-        cut = slice(s * 128, (s + 1) * 128)
-        layer = jnp.where(deep == 0, z_in[0, :, cut], 0.0)
-        layer = layer + jnp.where(deep == cz - 1, z_in[1, :, cut], 0.0)
-        base[s * per:(s + 1) * per] += DIFFUSION * layer.T.reshape(per, cy, cz)
+    if not merged:
+        finish_faces()
 
     for copy in arrivals + faces:
         copy.wait_send()
@@ -433,6 +499,14 @@
     for copy in backs:
         copy.wait()
     wall[...] = WALL_COUPLING * (ret[...] - outp[1:senders + 1])
+    if merged:
+        other = pl.ds(1 - me, 1)
+        wall[other] = wall[other] + WALL_COUPLING * sums[0, 0:1, :][None]
+        for side, has, _, _, _, _ in sides:
+            @pl.when(has)
+            def _():
+                for copy in far_copies(side):
+                    copy.wait_send()
 
 
 def finish(group, base, hot, src, wall, solid, new_h, solid_h, new, sems):
@@ -513,6 +587,9 @@
         pltpu.VMEM((3, 2 * tiles, width), F32),
         pltpu.VMEM((2, tiles, width), F32),
         pltpu.VMEM((2, REACH * width, 2 * REACH * width), BF16),
+        pltpu.VMEM((REACH * REACH, width, width), F32),
+        pltpu.VMEM((REACH * width, 2 * REACH * width), BF16),
+        pltpu.VMEM((senders, 1, width), F32),
         dma((8,)),
         dma((senders,)), dma((senders,)),
         dma((senders,)), dma((senders,)),
@@ -520,6 +597,7 @@
         dma((SWEEPS - 1, 2)), dma((SWEEPS - 1, 2)),
         dma((6,)), dma((6,)),
         pltpu.SemaphoreType.REGULAR,
+        dma((4,)), dma((4,)),
     ]
     parts = pl.pallas_call(
         functools.partial(kernel, senders, group),

time: 19.7 us -> 18.9 us (0.959)
  Pallas kernels: 18.9 us -> 18.1 us
    pallas_call x1, Pallas kernels: 17.8 us -> 17 us  [per_device(): pl.pallas_call(functools.partial(kernel, senders, group), out_shape=(pltp...]
where the time goes in v6:
time: 18.9 us; the launch traced here: 18.7 us
  Pallas kernels  18.1 us (96%)
  between operations  0.64 us (3%)
    pallas_call x1, Pallas kernels, per_device(): pl.pallas_call(functools.partial(kernel, senders, group), out_shape=(pltp...  17 us
    pallas_call x1, Pallas kernels, per_device(): pl.pallas_call(functools.partial(finish, group), out_shape=(jax.ShapeDtyp...  1.1 us

profile of v6, /device:TPU:0, one launch (start us, length us, event | category | flops | bytes accessed | tf_op | source)
XLA Modules:
  0.0 18.7 jit_solution(2915306545803904668)
XLA Ops:
  0.6 17.0 %shard_map.95 = (f32[16,64,128]{2,1,0:T(8,128)S(1)}, bf16[1,1024,256]{2,1,0:T(8,128)(2,1)S(1)}, s32[2,1,1,128]{3,2,1,0:T(1,128)S(1)}, f32[2,1,128]{2,1,0:T(1,128)S(1)}, f32[1,8,128]{2,1,0:T(8,128)S(1)}) custom-call(f32[16,64,128]{2,1,0:T(8,128)} %fluid_h.1, s32[16,64,128]{2,1,0:T(8,128)} %liquid_h.1, s32[2,1,1,128]{3,2,1,0:T(1,128)} %src_h.1, ...), custom_call_target="tpu_custom_call" | custom-call | tf_op jit(solution)/shard_map/pallas_call | solution.py:602
  17.6 1.1 %shard_map.96 = (f32[16,64,128]{2,1,0:T(8,128)}, f32[1,8,128]{2,1,0:T(8,128)}) custom-call(f32[16,64,128]{2,1,0:T(8,128)S(1)} %get-tuple-element.7.base, bf16[1,1024,256]{2,1,0:T(8,128)(2,1)S(1)} %get-tuple-element.8.hot, s32[2,1,1,128]{3,2,1,0:T(1,128)S(1)} %get-tuple-element.9.src, f32[2,1,128]{2,1,0:T(1,128)S(1)} %get-tuple-element.10.wall, ...), custom_call_target="tpu_custom_call" | custom-call | tf_op jit(solution)/shard_map/pallas_call | solution.py:619

commit v7 on v6

--- a/solution.py
+++ b/solution.py
@@ -312,11 +312,12 @@
         return [send(blocks.at[0, lo + j, o], far_in.at[n], far_send.at[n], far_recv.at[n],
                      {"gx": left if side == 0 else right}) for n, i, j, o in far_blocks(side)]
 
-    def send_far():
+    def send_far(turn):
         for side, has, _, _, _, _ in sides:
             @pl.when(has)
             def _():
-                for copy in far_copies(side):
+                copies = far_copies(side)
+                for copy in copies[:REACH] if turn == 0 else copies[REACH:]:
                     copy.start()
 
     def correct(scale_new):
@@ -434,13 +435,15 @@
     for k in range(SWEEPS - 1):
         rho_next = 1.0 / (4.0 - rho_old)
         ext[REACH:REACH + tiles, :] = iterate
-        if merged and k == 1:
-            send_far()
+        if merged and k < 2:
+            send_far(k)
         couple(0, local)
         part = right_side - diagonal * iterate - sums[0]
         if k == 0:
             loads[7].wait()
             stencil(0, cx // 2)
+        if k == 1:
+            stencil(cx // 2, cx)
 
             @pl.when(even)
             def _():
@@ -448,8 +451,6 @@
                 for face in faces[2:]:
                     face.start()
 
-        if k == 1:
-            stencil(cx // 2, cx)
         if merged and k == SWEEPS - 2:
             change = rho_next * rho_old * update + 4.0 * rho_next * inverse * part
             pick_back(iterate + change, sent)

time: 18.9 us -> 17.9 us (0.947)
  Pallas kernels: 18.1 us -> 17.1 us
    pallas_call x1, Pallas kernels: 17 us -> 16 us  [per_device(): pl.pallas_call(functools.partial(kernel, senders, group), out_shape=(pltp...]
where the time goes in v7:
time: 17.9 us; the launch traced here: 17.7 us
  Pallas kernels  17.1 us (96%)
  between operations  0.64 us (4%)
    pallas_call x1, Pallas kernels, per_device(): pl.pallas_call(functools.partial(kernel, senders, group), out_shape=(pltp...  16 us
    pallas_call x1, Pallas kernels, per_device(): pl.pallas_call(functools.partial(finish, group), out_shape=(jax.ShapeDtyp...  1.1 us

profile of v7, /device:TPU:0, one launch (start us, length us, event | category | flops | bytes accessed | tf_op | source)
XLA Modules:
  0.0 17.7 jit_solution(2438950644846132044)
XLA Ops:
  0.6 16.0 %shard_map.95 = (f32[16,64,128]{2,1,0:T(8,128)S(1)}, bf16[1,1024,256]{2,1,0:T(8,128)(2,1)S(1)}, s32[2,1,1,128]{3,2,1,0:T(1,128)S(1)}, f32[2,1,128]{2,1,0:T(1,128)S(1)}, f32[1,8,128]{2,1,0:T(8,128)S(1)}) custom-call(f32[16,64,128]{2,1,0:T(8,128)} %fluid_h.1, s32[16,64,128]{2,1,0:T(8,128)} %liquid_h.1, s32[2,1,1,128]{3,2,1,0:T(1,128)} %src_h.1, ...), custom_call_target="tpu_custom_call" | custom-call | tf_op jit(solution)/shard_map/pallas_call | solution.py:603
  16.6 1.1 %shard_map.96 = (f32[16,64,128]{2,1,0:T(8,128)}, f32[1,8,128]{2,1,0:T(8,128)}) custom-call(f32[16,64,128]{2,1,0:T(8,128)S(1)} %get-tuple-element.7.base, bf16[1,1024,256]{2,1,0:T(8,128)(2,1)S(1)} %get-tuple-element.8.hot, s32[2,1,1,128]{3,2,1,0:T(1,128)S(1)} %get-tuple-element.9.src, f32[2,1,128]{2,1,0:T(1,128)S(1)} %get-tuple-element.10.wall, ...), custom_call_target="tpu_custom_call" | custom-call | tf_op jit(solution)/shard_map/pallas_call | solution.py:620

commit v8 on v7

--- a/solution.py
+++ b/solution.py
@@ -269,6 +269,8 @@
     every = list(range(NB))
     middle = [(t, every) for t in range(REACH, tiles - REACH)]
     local = [(t, [o for o in every if inside(t, o)]) for t in range(tiles)]
+    from_first = [(t, [o for o in offsets if t + o < 2 * REACH]) for t, offsets in local[:2 * REACH]]
+    from_last = [(t, [o for o in offsets if t + o >= tiles]) for t, offsets in local[tiles - 2 * REACH:]]
     first = [(t, every) for t in range(REACH)]
     last = [(t, every) for t in range(tiles - REACH, tiles)]
     no_left, no_right = jnp.logical_not(has_left), jnp.logical_not(has_right)
@@ -437,8 +439,16 @@
         ext[REACH:REACH + tiles, :] = iterate
         if merged and k < 2:
             send_far(k)
-        couple(0, local)
-        part = right_side - diagonal * iterate - sums[0]
+        if k == SWEEPS - 2:
+            ext[REACH:REACH + tiles, :] = delta
+            for has, touched in ((has_left, from_first), (has_right, from_last)):
+                @pl.when(has)
+                def _():
+                    couple(2, touched)
+            part = right_side - diagonal * iterate - (ahead + sums[2])
+        else:
+            couple(0, local)
+            part = right_side - diagonal * iterate - sums[0]
         if k == 0:
             loads[7].wait()
             stencil(0, cx // 2)
@@ -466,7 +476,12 @@
                 finish_faces()
         if k == 0:
             make_edges()
+        if k == SWEEPS - 3:
+            ext[REACH:REACH + tiles, :] = iterate + rho_next * rho_old * update + 4.0 * rho_next * inverse * part
+            couple(0, local)
+            ahead = sums[0]
         take(k, part, rho_next * rho_old, 4.0 * rho_next)
+        delta = -4.0 * rho_next * inverse * sums[1]
         residual = part - sums[1]
         update = rho_next * rho_old * update + 4.0 * rho_next * inverse * residual
         iterate = iterate + update
@@ -586,7 +601,7 @@
         pltpu.VMEM((2, 1, rows), F32),
         pltpu.VMEM((ext_rows, width), F32),
         pltpu.VMEM((3, 2 * tiles, width), F32),
-        pltpu.VMEM((2, tiles, width), F32),
+        pltpu.VMEM((3, tiles, width), F32),
         pltpu.VMEM((2, REACH * width, 2 * REACH * width), BF16),
         pltpu.VMEM((REACH * REACH, width, width), F32),
         pltpu.VMEM((REACH * width, 2 * REACH * width), BF16),

time: 17.9 us -> 17.8 us (level)
  no operation moved by 1% of the time
where the time goes in v8:
time: 17.8 us; the launch traced here: 17.6 us
  Pallas kernels  17 us (96%)
  between operations  0.64 us (4%)
    pallas_call x1, Pallas kernels, per_device(): pl.pallas_call(functools.partial(kernel, senders, group), out_shape=(pltp...  15.9 us
    pallas_call x1, Pallas kernels, per_device(): pl.pallas_call(functools.partial(finish, group), out_shape=(jax.ShapeDtyp...  1.1 us

profile of v8, /device:TPU:0, one launch (start us, length us, event | category | flops | bytes accessed | tf_op | source)
XLA Modules:
  0.0 17.6 jit_solution(4901615924215375431)
XLA Ops:
  0.6 15.9 %shard_map.95 = (f32[16,64,128]{2,1,0:T(8,128)S(1)}, bf16[1,1024,256]{2,1,0:T(8,128)(2,1)S(1)}, s32[2,1,1,128]{3,2,1,0:T(1,128)S(1)}, f32[2,1,128]{2,1,0:T(1,128)S(1)}, f32[1,8,128]{2,1,0:T(8,128)S(1)}) custom-call(f32[16,64,128]{2,1,0:T(8,128)} %fluid_h.1, s32[16,64,128]{2,1,0:T(8,128)} %liquid_h.1, s32[2,1,1,128]{3,2,1,0:T(1,128)} %src_h.1, ...), custom_call_target="tpu_custom_call" | custom-call | tf_op jit(solution)/shard_map/pallas_call | solution.py:618
  16.5 1.1 %shard_map.96 = (f32[16,64,128]{2,1,0:T(8,128)}, f32[1,8,128]{2,1,0:T(8,128)}) custom-call(f32[16,64,128]{2,1,0:T(8,128)S(1)} %get-tuple-element.7.base, bf16[1,1024,256]{2,1,0:T(8,128)(2,1)S(1)} %get-tuple-element.8.hot, s32[2,1,1,128]{3,2,1,0:T(1,128)S(1)} %get-tuple-element.9.src, f32[2,1,128]{2,1,0:T(1,128)S(1)} %get-tuple-element.10.wall, ...), custom_call_target="tpu_custom_call" | custom-call | tf_op jit(solution)/shard_map/pallas_call | solution.py:635
